TPU v7x, 256 devices: a whole 4x4x8 slice. The times are simulated.
256 devices in a mesh: grp: 16 (over x_lo, y, core), blk: 16 (over x_hi, z).
Axes of the slice: x: 4 (x_hi: 2, x_lo: 2; x = x_hi * 2 + x_lo), y: 4, z: 8, core: 2. Of those that a mesh axis runs over, the one named last changes fastest.
Arguments:
- image_raw: bfloat16 [16384, 1152], P(('grp', 'blk')), may hold values from -1 to 1
- text_raw: bfloat16 [16384, 1152], P(('grp', 'blk')), may hold values from -1 to 1
- log_scale: float32 [1], replicated, may hold values from 1.6 to 2.6
- bias: float32 [1], replicated, may hold values from -5 to -2.5
Outputs:
- grad_image: bfloat16 [16384, 1152], P(('grp', 'blk'))
- grad_text: bfloat16 [16384, 1152], P(('grp', 'blk'))
All inputs are finite; a program needn't handle non-finite values.
Results may differ from a plain program's by a relative error of at most 0.0069.
Values may be sent and summed in bfloat16 or wider, within the bound.
A program may use at most 64 MiB of HBM per device.

v0:
```python
import jax
import jax.numpy as jnp
from jax import lax
from jax.sharding import PartitionSpec as P


def from_behind(value, axis, steps):
    count = lax.axis_size(axis)
    pairs = [(source, (source + steps) % count) for source in range(count)]
    return lax.ppermute(value, axis, pairs)


def normalize(raw):
    values = raw.astype(jnp.float32)
    inverse = lax.rsqrt(jnp.sum(values * values, axis=-1, keepdims=True) + 1e-06)
    return (values * inverse, inverse)


def tangent(back, unit, inverse):
    along = jnp.sum(unit * back, axis=-1, keepdims=True)
    return ((back - unit * along) * inverse).astype(jnp.bfloat16)


def pair_tile(images, text_block, scale, offset, home, step_no):
    logits = (
        scale
        * lax.dot_general(
            images, text_block, (((1,), (1,)), ((), ())), preferred_element_type=jnp.float32
        )
        + offset
    )
    rows = lax.broadcasted_iota(jnp.int32, logits.shape, 0)
    cols = lax.broadcasted_iota(jnp.int32, logits.shape, 1)
    diagonal = jnp.logical_and(rows == home + cols, step_no == 0)
    weight = (jax.nn.sigmoid(logits) - diagonal.astype(jnp.float32)).astype(jnp.bfloat16)
    image_add = scale * jnp.dot(weight, text_block, preferred_element_type=jnp.float32)
    text_add = scale * lax.dot_general(
        weight, images, (((0,), (0,)), ((), ())), preferred_element_type=jnp.float32
    )
    return (image_add, text_add)


def per_device(image_raw, text_raw, log_scale, bias):
    scale = jnp.exp(log_scale[0])
    offset = bias[0]
    image_unit, image_inv = normalize(image_raw)
    text_unit, text_inv = normalize(text_raw)
    image_half = image_unit.astype(jnp.bfloat16)
    text_half = text_unit.astype(jnp.bfloat16)
    images = lax.all_gather(image_half, "grp", axis=0, tiled=True)
    rows_dev = image_raw.shape[0]
    width = image_raw.shape[1]
    home = lax.axis_index("grp") * rows_dev
    length = lax.axis_size("blk")
    image_empty = jnp.zeros(images.shape, jnp.float32)

    def turn(step_no, state):
        image_acc, text_block, text_acc = state
        image_add, text_add = pair_tile(images, text_block, scale, offset, home, step_no)
        text_block, text_acc = (
            from_behind(text_block.astype(jnp.float32), "blk", 1).astype(text_block.dtype),
            from_behind(text_acc + text_add, "blk", 1),
        )
        return (image_acc + image_add, text_block, text_acc)

    start = (image_empty, text_half, jnp.zeros((rows_dev, width), jnp.float32))
    image_acc, unused_text, text_back = lax.fori_loop(0, length, turn, start)
    image_back = lax.psum_scatter(image_acc, "grp", scatter_dimension=0, tiled=True)
    return (tangent(image_back, image_unit, image_inv), tangent(text_back, text_unit, text_inv))


def solution(mesh):
    in_specs = (P(("grp", "blk"), None), P(("grp", "blk"), None), P(), P())
    out_specs = (P(("grp", "blk"), None), P(("grp", "blk"), None))
    return jax.shard_map(
        per_device, mesh=mesh, in_specs=in_specs, out_specs=out_specs, check_vma=False
    )
```

profile of v0, /device:TPU:1, one launch (start us, length us, event | category | flops | bytes accessed | tf_op | source)
XLA Modules:
  0.0 383.1 jit_solution(15898032509806091390)
XLA Ops:
  12.8 38.8 %all-gather.2.cloned.1.call-done = bf16[1024,1152]{1,0:T(8,128)(2,1)} async-done(((bf16[64,1152]{1,0:T(8,128)(2,1)}), bf16[1024,1152]{1,0:T(8,128)(2,1)}) %all-gather.2.cloned.1.call-update) | async-done | bytes 2359312 | tf_op jit(solution)/shard_map/all_gather | solution.py:50
  51.6 256.0 %while.18 = (s32[]{:T(128)}, f32[1024,1152]{1,0:T(8,128)}, bf16[64,1152]{1,0:T(8,128)(2,1)S(1)}, f32[64,1152]{1,0:T(8,128)S(1)}, f32[]{:T(128)}, /*index=5*/bf16...) while((s32[]{:T(128)}, f32[1024,1152]{1,0:T(8,128)}, ...), condition=%wide.region_3.0_spmd.clone, body=%wide.region_2.0_spmd.clone.sunk | while | flops 457326656 | bytes 17498836 | solution.py:67
  62.7 7.4 %collective-permute-done.1 = f32[64,1152]{1,0:T(8,128)S(1)} collective-permute-done((f32[64,1152]{1,0:T(8,128)S(1)}, f32[64,1152]{1,0:T(8,128)S(1)}, u32[]{:S(2)}, u32[]{:S(2)}) %collective-permute-start.1) | collective-permute-done | bytes 294944 | tf_op jit(solution)/shard_map/while/body/eval_jaxpr/ppermute | solution.py:10
  75.7 5.3 %fusion.48 = f32[1024,1152]{1,0:T(8,128)} fusion(bf16[1024,64]{0,1:T(8,128)(2,1)S(1)} %fusion.47, bf16[64,1152]{1,0:T(8,128)(2,1)S(1)} %copy.12, f32[1024,1152]{1,0:T(8,128)} %get-tuple-element.247, f32[]{:T(128)} %get-tuple-element.260, pred[]{:T(512)S(6)} %compare.3), kind=kOutput, calls=%fused_computation.1.clone.1 | convolution fusion | flops 154533888 | bytes 9715717 | tf_op jit(solution)/shard_map/while/body/eval_jaxpr/dot_general | solution.py:36
  81.0 5.4 %collective-permute-done.1 = f32[64,1152]{1,0:T(8,128)S(1)} collective-permute-done((f32[64,1152]{1,0:T(8,128)S(1)}, f32[64,1152]{1,0:T(8,128)S(1)}, u32[]{:S(2)}, u32[]{:S(2)}) %collective-permute-start.1) | collective-permute-done | bytes 294944 | tf_op jit(solution)/shard_map/while/body/eval_jaxpr/ppermute | solution.py:10
  92.0 5.3 %fusion.48 = f32[1024,1152]{1,0:T(8,128)} fusion(bf16[1024,64]{0,1:T(8,128)(2,1)S(1)} %fusion.47, bf16[64,1152]{1,0:T(8,128)(2,1)S(1)} %copy.12, f32[1024,1152]{1,0:T(8,128)} %get-tuple-element.247, f32[]{:T(128)} %get-tuple-element.260, pred[]{:T(512)S(6)} %compare.3), kind=kOutput, calls=%fused_computation.1.clone.1 | convolution fusion | flops 154533888 | bytes 9715717 | tf_op jit(solution)/shard_map/while/body/eval_jaxpr/dot_general | solution.py:36
  107.4 5.3 %fusion.48 = f32[1024,1152]{1,0:T(8,128)} fusion(bf16[1024,64]{0,1:T(8,128)(2,1)S(1)} %fusion.47, bf16[64,1152]{1,0:T(8,128)(2,1)S(1)} %copy.12, f32[1024,1152]{1,0:T(8,128)} %get-tuple-element.247, f32[]{:T(128)} %get-tuple-element.260, pred[]{:T(512)S(6)} %compare.3), kind=kOutput, calls=%fused_computation.1.clone.1 | convolution fusion | flops 154533888 | bytes 9715717 | tf_op jit(solution)/shard_map/while/body/eval_jaxpr/dot_general | solution.py:36
  122.2 5.3 %fusion.48 = f32[1024,1152]{1,0:T(8,128)} fusion(bf16[1024,64]{0,1:T(8,128)(2,1)S(1)} %fusion.47, bf16[64,1152]{1,0:T(8,128)(2,1)S(1)} %copy.12, f32[1024,1152]{1,0:T(8,128)} %get-tuple-element.247, f32[]{:T(128)} %get-tuple-element.260, pred[]{:T(512)S(6)} %compare.3), kind=kOutput, calls=%fused_computation.1.clone.1 | convolution fusion | flops 154533888 | bytes 9715717 | tf_op jit(solution)/shard_map/while/body/eval_jaxpr/dot_general | solution.py:36
  127.4 4.8 %collective-permute-done.1 = f32[64,1152]{1,0:T(8,128)S(1)} collective-permute-done((f32[64,1152]{1,0:T(8,128)S(1)}, f32[64,1152]{1,0:T(8,128)S(1)}, u32[]{:S(2)}, u32[]{:S(2)}) %collective-permute-start.1) | collective-permute-done | bytes 294944 | tf_op jit(solution)/shard_map/while/body/eval_jaxpr/ppermute | solution.py:10
  137.9 5.3 %fusion.48 = f32[1024,1152]{1,0:T(8,128)} fusion(bf16[1024,64]{0,1:T(8,128)(2,1)S(1)} %fusion.47, bf16[64,1152]{1,0:T(8,128)(2,1)S(1)} %copy.12, f32[1024,1152]{1,0:T(8,128)} %get-tuple-element.247, f32[]{:T(128)} %get-tuple-element.260, pred[]{:T(512)S(6)} %compare.3), kind=kOutput, calls=%fused_computation.1.clone.1 | convolution fusion | flops 154533888 | bytes 9715717 | tf_op jit(solution)/shard_map/while/body/eval_jaxpr/dot_general | solution.py:36
  143.2 5.0 %collective-permute-done.1 = f32[64,1152]{1,0:T(8,128)S(1)} collective-permute-done((f32[64,1152]{1,0:T(8,128)S(1)}, f32[64,1152]{1,0:T(8,128)S(1)}, u32[]{:S(2)}, u32[]{:S(2)}) %collective-permute-start.1) | collective-permute-done | bytes 294944 | tf_op jit(solution)/shard_map/while/body/eval_jaxpr/ppermute | solution.py:10
  153.8 5.3 %fusion.48 = f32[1024,1152]{1,0:T(8,128)} fusion(bf16[1024,64]{0,1:T(8,128)(2,1)S(1)} %fusion.47, bf16[64,1152]{1,0:T(8,128)(2,1)S(1)} %copy.12, f32[1024,1152]{1,0:T(8,128)} %get-tuple-element.247, f32[]{:T(128)} %get-tuple-element.260, pred[]{:T(512)S(6)} %compare.3), kind=kOutput, calls=%fused_computation.1.clone.1 | convolution fusion | flops 154533888 | bytes 9715717 | tf_op jit(solution)/shard_map/while/body/eval_jaxpr/dot_general | solution.py:36
  159.1 5.0 %collective-permute-done.1 = f32[64,1152]{1,0:T(8,128)S(1)} collective-permute-done((f32[64,1152]{1,0:T(8,128)S(1)}, f32[64,1152]{1,0:T(8,128)S(1)}, u32[]{:S(2)}, u32[]{:S(2)}) %collective-permute-start.1) | collective-permute-done | bytes 294944 | tf_op jit(solution)/shard_map/while/body/eval_jaxpr/ppermute | solution.py:10
  169.8 5.3 %fusion.48 = f32[1024,1152]{1,0:T(8,128)} fusion(bf16[1024,64]{0,1:T(8,128)(2,1)S(1)} %fusion.47, bf16[64,1152]{1,0:T(8,128)(2,1)S(1)} %copy.12, f32[1024,1152]{1,0:T(8,128)} %get-tuple-element.247, f32[]{:T(128)} %get-tuple-element.260, pred[]{:T(512)S(6)} %compare.3), kind=kOutput, calls=%fused_computation.1.clone.1 | convolution fusion | flops 154533888 | bytes 9715717 | tf_op jit(solution)/shard_map/while/body/eval_jaxpr/dot_general | solution.py:36
  175.1 5.0 %collective-permute-done.1 = f32[64,1152]{1,0:T(8,128)S(1)} collective-permute-done((f32[64,1152]{1,0:T(8,128)S(1)}, f32[64,1152]{1,0:T(8,128)S(1)}, u32[]{:S(2)}, u32[]{:S(2)}) %collective-permute-start.1) | collective-permute-done | bytes 294944 | tf_op jit(solution)/shard_map/while/body/eval_jaxpr/ppermute | solution.py:10
  185.7 5.3 %fusion.48 = f32[1024,1152]{1,0:T(8,128)} fusion(bf16[1024,64]{0,1:T(8,128)(2,1)S(1)} %fusion.47, bf16[64,1152]{1,0:T(8,128)(2,1)S(1)} %copy.12, f32[1024,1152]{1,0:T(8,128)} %get-tuple-element.247, f32[]{:T(128)} %get-tuple-element.260, pred[]{:T(512)S(6)} %compare.3), kind=kOutput, calls=%fused_computation.1.clone.1 | convolution fusion | flops 154533888 | bytes 9715717 | tf_op jit(solution)/shard_map/while/body/eval_jaxpr/dot_general | solution.py:36
  191.0 5.0 %collective-permute-done.1 = f32[64,1152]{1,0:T(8,128)S(1)} collective-permute-done((f32[64,1152]{1,0:T(8,128)S(1)}, f32[64,1152]{1,0:T(8,128)S(1)}, u32[]{:S(2)}, u32[]{:S(2)}) %collective-permute-start.1) | collective-permute-done | bytes 294944 | tf_op jit(solution)/shard_map/while/body/eval_jaxpr/ppermute | solution.py:10
  201.7 5.3 %fusion.48 = f32[1024,1152]{1,0:T(8,128)} fusion(bf16[1024,64]{0,1:T(8,128)(2,1)S(1)} %fusion.47, bf16[64,1152]{1,0:T(8,128)(2,1)S(1)} %copy.12, f32[1024,1152]{1,0:T(8,128)} %get-tuple-element.247, f32[]{:T(128)} %get-tuple-element.260, pred[]{:T(512)S(6)} %compare.3), kind=kOutput, calls=%fused_computation.1.clone.1 | convolution fusion | flops 154533888 | bytes 9715717 | tf_op jit(solution)/shard_map/while/body/eval_jaxpr/dot_general | solution.py:36
  206.9 5.0 %collective-permute-done.1 = f32[64,1152]{1,0:T(8,128)S(1)} collective-permute-done((f32[64,1152]{1,0:T(8,128)S(1)}, f32[64,1152]{1,0:T(8,128)S(1)}, u32[]{:S(2)}, u32[]{:S(2)}) %collective-permute-start.1) | collective-permute-done | bytes 294944 | tf_op jit(solution)/shard_map/while/body/eval_jaxpr/ppermute | solution.py:10
  217.6 5.3 %fusion.48 = f32[1024,1152]{1,0:T(8,128)} fusion(bf16[1024,64]{0,1:T(8,128)(2,1)S(1)} %fusion.47, bf16[64,1152]{1,0:T(8,128)(2,1)S(1)} %copy.12, f32[1024,1152]{1,0:T(8,128)} %get-tuple-element.247, f32[]{:T(128)} %get-tuple-element.260, pred[]{:T(512)S(6)} %compare.3), kind=kOutput, calls=%fused_computation.1.clone.1 | convolution fusion | flops 154533888 | bytes 9715717 | tf_op jit(solution)/shard_map/while/body/eval_jaxpr/dot_general | solution.py:36
  222.9 5.0 %collective-permute-done.1 = f32[64,1152]{1,0:T(8,128)S(1)} collective-permute-done((f32[64,1152]{1,0:T(8,128)S(1)}, f32[64,1152]{1,0:T(8,128)S(1)}, u32[]{:S(2)}, u32[]{:S(2)}) %collective-permute-start.1) | collective-permute-done | bytes 294944 | tf_op jit(solution)/shard_map/while/body/eval_jaxpr/ppermute | solution.py:10
  233.5 5.3 %fusion.48 = f32[1024,1152]{1,0:T(8,128)} fusion(bf16[1024,64]{0,1:T(8,128)(2,1)S(1)} %fusion.47, bf16[64,1152]{1,0:T(8,128)(2,1)S(1)} %copy.12, f32[1024,1152]{1,0:T(8,128)} %get-tuple-element.247, f32[]{:T(128)} %get-tuple-element.260, pred[]{:T(512)S(6)} %compare.3), kind=kOutput, calls=%fused_computation.1.clone.1 | convolution fusion | flops 154533888 | bytes 9715717 | tf_op jit(solution)/shard_map/while/body/eval_jaxpr/dot_general | solution.py:36
  238.8 5.0 %collective-permute-done.1 = f32[64,1152]{1,0:T(8,128)S(1)} collective-permute-done((f32[64,1152]{1,0:T(8,128)S(1)}, f32[64,1152]{1,0:T(8,128)S(1)}, u32[]{:S(2)}, u32[]{:S(2)}) %collective-permute-start.1) | collective-permute-done | bytes 294944 | tf_op jit(solution)/shard_map/while/body/eval_jaxpr/ppermute | solution.py:10
  249.5 5.3 %fusion.48 = f32[1024,1152]{1,0:T(8,128)} fusion(bf16[1024,64]{0,1:T(8,128)(2,1)S(1)} %fusion.47, bf16[64,1152]{1,0:T(8,128)(2,1)S(1)} %copy.12, f32[1024,1152]{1,0:T(8,128)} %get-tuple-element.247, f32[]{:T(128)} %get-tuple-element.260, pred[]{:T(512)S(6)} %compare.3), kind=kOutput, calls=%fused_computation.1.clone.1 | convolution fusion | flops 154533888 | bytes 9715717 | tf_op jit(solution)/shard_map/while/body/eval_jaxpr/dot_general | solution.py:36
  254.8 5.0 %collective-permute-done.1 = f32[64,1152]{1,0:T(8,128)S(1)} collective-permute-done((f32[64,1152]{1,0:T(8,128)S(1)}, f32[64,1152]{1,0:T(8,128)S(1)}, u32[]{:S(2)}, u32[]{:S(2)}) %collective-permute-start.1) | collective-permute-done | bytes 294944 | tf_op jit(solution)/shard_map/while/body/eval_jaxpr/ppermute | solution.py:10
  265.4 5.3 %fusion.48 = f32[1024,1152]{1,0:T(8,128)} fusion(bf16[1024,64]{0,1:T(8,128)(2,1)S(1)} %fusion.47, bf16[64,1152]{1,0:T(8,128)(2,1)S(1)} %copy.12, f32[1024,1152]{1,0:T(8,128)} %get-tuple-element.247, f32[]{:T(128)} %get-tuple-element.260, pred[]{:T(512)S(6)} %compare.3), kind=kOutput, calls=%fused_computation.1.clone.1 | convolution fusion | flops 154533888 | bytes 9715717 | tf_op jit(solution)/shard_map/while/body/eval_jaxpr/dot_general | solution.py:36
  270.7 5.0 %collective-permute-done.1 = f32[64,1152]{1,0:T(8,128)S(1)} collective-permute-done((f32[64,1152]{1,0:T(8,128)S(1)}, f32[64,1152]{1,0:T(8,128)S(1)}, u32[]{:S(2)}, u32[]{:S(2)}) %collective-permute-start.1) | collective-permute-done | bytes 294944 | tf_op jit(solution)/shard_map/while/body/eval_jaxpr/ppermute | solution.py:10
  281.4 5.3 %fusion.48 = f32[1024,1152]{1,0:T(8,128)} fusion(bf16[1024,64]{0,1:T(8,128)(2,1)S(1)} %fusion.47, bf16[64,1152]{1,0:T(8,128)(2,1)S(1)} %copy.12, f32[1024,1152]{1,0:T(8,128)} %get-tuple-element.247, f32[]{:T(128)} %get-tuple-element.260, pred[]{:T(512)S(6)} %compare.3), kind=kOutput, calls=%fused_computation.1.clone.1 | convolution fusion | flops 154533888 | bytes 9715717 | tf_op jit(solution)/shard_map/while/body/eval_jaxpr/dot_general | solution.py:36
  286.6 5.0 %collective-permute-done.1 = f32[64,1152]{1,0:T(8,128)S(1)} collective-permute-done((f32[64,1152]{1,0:T(8,128)S(1)}, f32[64,1152]{1,0:T(8,128)S(1)}, u32[]{:S(2)}, u32[]{:S(2)}) %collective-permute-start.1) | collective-permute-done | bytes 294944 | tf_op jit(solution)/shard_map/while/body/eval_jaxpr/ppermute | solution.py:10
  297.3 5.3 %fusion.48 = f32[1024,1152]{1,0:T(8,128)} fusion(bf16[1024,64]{0,1:T(8,128)(2,1)S(1)} %fusion.47, bf16[64,1152]{1,0:T(8,128)(2,1)S(1)} %copy.12, f32[1024,1152]{1,0:T(8,128)} %get-tuple-element.247, f32[]{:T(128)} %get-tuple-element.260, pred[]{:T(512)S(6)} %compare.3), kind=kOutput, calls=%fused_computation.1.clone.1 | convolution fusion | flops 154533888 | bytes 9715717 | tf_op jit(solution)/shard_map/while/body/eval_jaxpr/dot_general | solution.py:36
  302.6 5.0 %collective-permute-done.1 = f32[64,1152]{1,0:T(8,128)S(1)} collective-permute-done((f32[64,1152]{1,0:T(8,128)S(1)}, f32[64,1152]{1,0:T(8,128)S(1)}, u32[]{:S(2)}, u32[]{:S(2)}) %collective-permute-start.1) | collective-permute-done | bytes 294944 | tf_op jit(solution)/shard_map/while/body/eval_jaxpr/ppermute | solution.py:10
  309.5 63.8 %reduce-scatter.2.cloned.1.call-done = f32[64,1152]{1,0:T(8,128)} async-done(((f32[1024,1152]{1,0:T(8,128)}), f32[64,1152]{1,0:T(8,128)}) %reduce-scatter.2.cloned.1.call-update) | async-done | bytes 294928 | tf_op jit(solution)/shard_map/reduce_scatter | solution.py:68
  (135 shorter events, 112.7 us)
Async XLA Ops:
  7.2 44.4 %all-gather.2.cloned.1.call-start = ((), (), s32[]{:S(2)}) async-start(), calls=%async_computation.1 | async-start | bytes 2506752 | tf_op jit(solution)/shard_map/all_gather | solution.py:50
  10.0 363.4 %reduce-scatter.2.cloned.1.call-start = ((), (), s32[]{:S(2)}) async-start(), calls=%async_computation.2 | async-start | bytes 5013504 | tf_op jit(solution)/shard_map/reduce_scatter | solution.py:68
  51.6 11.0 %collective-permute-start = (bf16[64,1152]{1,0:T(8,128)(2,1)S(1)}, bf16[64,1152]{1,0:T(8,128)(2,1)S(1)}, u32[]{:S(2)}, u32[]{:S(2)}) collective-permute-start(bf16[64,1152]{1,0:T(8,128)(2,1)S(1)} %copy.12), channel_id=1, source_target_pairs={{0,1},{1,2},{2,3},{3,4},{4,5},{5,6},{6,7},{7,8},{8,9},{9,10},{10,1... | collective-permute-start | bytes 442376 | tf_op jit(solution)/shard_map/while/body/eval_jaxpr/ppermute | solution.py:10
  58.4 11.7 %collective-permute-start.1 = (f32[64,1152]{1,0:T(8,128)S(1)}, f32[64,1152]{1,0:T(8,128)S(1)}, u32[]{:S(2)}, u32[]{:S(2)}) collective-permute-start(f32[64,1152]{1,0:T(8,128)S(1)} %fusion.49), channel_id=1, source_target_pairs={{0,1},{1,2},{2,3},{3,4},{4,5},{5,6},{6,7},{7,8},{8,9},{9,10},{10,1... | collective-permute-start | bytes 884744 | tf_op jit(solution)/shard_map/while/body/eval_jaxpr/ppermute | solution.py:10
  70.1 10.9 %collective-permute-start = (bf16[64,1152]{1,0:T(8,128)(2,1)S(1)}, bf16[64,1152]{1,0:T(8,128)(2,1)S(1)}, u32[]{:S(2)}, u32[]{:S(2)}) collective-permute-start(bf16[64,1152]{1,0:T(8,128)(2,1)S(1)} %copy.12), channel_id=1, source_target_pairs={{0,1},{1,2},{2,3},{3,4},{4,5},{5,6},{6,7},{7,8},{8,9},{9,10},{10,1... | collective-permute-start | bytes 442376 | tf_op jit(solution)/shard_map/while/body/eval_jaxpr/ppermute | solution.py:10
  75.6 10.8 %collective-permute-start.1 = (f32[64,1152]{1,0:T(8,128)S(1)}, f32[64,1152]{1,0:T(8,128)S(1)}, u32[]{:S(2)}, u32[]{:S(2)}) collective-permute-start(f32[64,1152]{1,0:T(8,128)S(1)} %fusion.49), channel_id=1, source_target_pairs={{0,1},{1,2},{2,3},{3,4},{4,5},{5,6},{6,7},{7,8},{8,9},{9,10},{10,1... | collective-permute-start | bytes 884744 | tf_op jit(solution)/shard_map/while/body/eval_jaxpr/ppermute | solution.py:10
  86.4 10.9 %collective-permute-start = (bf16[64,1152]{1,0:T(8,128)(2,1)S(1)}, bf16[64,1152]{1,0:T(8,128)(2,1)S(1)}, u32[]{:S(2)}, u32[]{:S(2)}) collective-permute-start(bf16[64,1152]{1,0:T(8,128)(2,1)S(1)} %copy.12), channel_id=1, source_target_pairs={{0,1},{1,2},{2,3},{3,4},{4,5},{5,6},{6,7},{7,8},{8,9},{9,10},{10,1... | collective-permute-start | bytes 442376 | tf_op jit(solution)/shard_map/while/body/eval_jaxpr/ppermute | solution.py:10
  101.8 10.9 %collective-permute-start = (bf16[64,1152]{1,0:T(8,128)(2,1)S(1)}, bf16[64,1152]{1,0:T(8,128)(2,1)S(1)}, u32[]{:S(2)}, u32[]{:S(2)}) collective-permute-start(bf16[64,1152]{1,0:T(8,128)(2,1)S(1)} %copy.12), channel_id=1, source_target_pairs={{0,1},{1,2},{2,3},{3,4},{4,5},{5,6},{6,7},{7,8},{8,9},{9,10},{10,1... | collective-permute-start | bytes 442376 | tf_op jit(solution)/shard_map/while/body/eval_jaxpr/ppermute | solution.py:10
  116.6 10.9 %collective-permute-start = (bf16[64,1152]{1,0:T(8,128)(2,1)S(1)}, bf16[64,1152]{1,0:T(8,128)(2,1)S(1)}, u32[]{:S(2)}, u32[]{:S(2)}) collective-permute-start(bf16[64,1152]{1,0:T(8,128)(2,1)S(1)} %copy.12), channel_id=1, source_target_pairs={{0,1},{1,2},{2,3},{3,4},{4,5},{5,6},{6,7},{7,8},{8,9},{9,10},{10,1... | collective-permute-start | bytes 442376 | tf_op jit(solution)/shard_map/while/body/eval_jaxpr/ppermute | solution.py:10
  122.1 10.2 %collective-permute-start.1 = (f32[64,1152]{1,0:T(8,128)S(1)}, f32[64,1152]{1,0:T(8,128)S(1)}, u32[]{:S(2)}, u32[]{:S(2)}) collective-permute-start(f32[64,1152]{1,0:T(8,128)S(1)} %fusion.49), channel_id=1, source_target_pairs={{0,1},{1,2},{2,3},{3,4},{4,5},{5,6},{6,7},{7,8},{8,9},{9,10},{10,1... | collective-permute-start | bytes 884744 | tf_op jit(solution)/shard_map/while/body/eval_jaxpr/ppermute | solution.py:10
  132.3 10.9 %collective-permute-start = (bf16[64,1152]{1,0:T(8,128)(2,1)S(1)}, bf16[64,1152]{1,0:T(8,128)(2,1)S(1)}, u32[]{:S(2)}, u32[]{:S(2)}) collective-permute-start(bf16[64,1152]{1,0:T(8,128)(2,1)S(1)} %copy.12), channel_id=1, source_target_pairs={{0,1},{1,2},{2,3},{3,4},{4,5},{5,6},{6,7},{7,8},{8,9},{9,10},{10,1... | collective-permute-start | bytes 442376 | tf_op jit(solution)/shard_map/while/body/eval_jaxpr/ppermute | solution.py:10
  137.8 10.4 %collective-permute-start.1 = (f32[64,1152]{1,0:T(8,128)S(1)}, f32[64,1152]{1,0:T(8,128)S(1)}, u32[]{:S(2)}, u32[]{:S(2)}) collective-permute-start(f32[64,1152]{1,0:T(8,128)S(1)} %fusion.49), channel_id=1, source_target_pairs={{0,1},{1,2},{2,3},{3,4},{4,5},{5,6},{6,7},{7,8},{8,9},{9,10},{10,1... | collective-permute-start | bytes 884744 | tf_op jit(solution)/shard_map/while/body/eval_jaxpr/ppermute | solution.py:10
  148.2 10.9 %collective-permute-start = (bf16[64,1152]{1,0:T(8,128)(2,1)S(1)}, bf16[64,1152]{1,0:T(8,128)(2,1)S(1)}, u32[]{:S(2)}, u32[]{:S(2)}) collective-permute-start(bf16[64,1152]{1,0:T(8,128)(2,1)S(1)} %copy.12), channel_id=1, source_target_pairs={{0,1},{1,2},{2,3},{3,4},{4,5},{5,6},{6,7},{7,8},{8,9},{9,10},{10,1... | collective-permute-start | bytes 442376 | tf_op jit(solution)/shard_map/while/body/eval_jaxpr/ppermute | solution.py:10
  153.7 10.4 %collective-permute-start.1 = (f32[64,1152]{1,0:T(8,128)S(1)}, f32[64,1152]{1,0:T(8,128)S(1)}, u32[]{:S(2)}, u32[]{:S(2)}) collective-permute-start(f32[64,1152]{1,0:T(8,128)S(1)} %fusion.49), channel_id=1, source_target_pairs={{0,1},{1,2},{2,3},{3,4},{4,5},{5,6},{6,7},{7,8},{8,9},{9,10},{10,1... | collective-permute-start | bytes 884744 | tf_op jit(solution)/shard_map/while/body/eval_jaxpr/ppermute | solution.py:10
  164.2 10.9 %collective-permute-start = (bf16[64,1152]{1,0:T(8,128)(2,1)S(1)}, bf16[64,1152]{1,0:T(8,128)(2,1)S(1)}, u32[]{:S(2)}, u32[]{:S(2)}) collective-permute-start(bf16[64,1152]{1,0:T(8,128)(2,1)S(1)} %copy.12), channel_id=1, source_target_pairs={{0,1},{1,2},{2,3},{3,4},{4,5},{5,6},{6,7},{7,8},{8,9},{9,10},{10,1... | collective-permute-start | bytes 442376 | tf_op jit(solution)/shard_map/while/body/eval_jaxpr/ppermute | solution.py:10
  169.7 10.4 %collective-permute-start.1 = (f32[64,1152]{1,0:T(8,128)S(1)}, f32[64,1152]{1,0:T(8,128)S(1)}, u32[]{:S(2)}, u32[]{:S(2)}) collective-permute-start(f32[64,1152]{1,0:T(8,128)S(1)} %fusion.49), channel_id=1, source_target_pairs={{0,1},{1,2},{2,3},{3,4},{4,5},{5,6},{6,7},{7,8},{8,9},{9,10},{10,1... | collective-permute-start | bytes 884744 | tf_op jit(solution)/shard_map/while/body/eval_jaxpr/ppermute | solution.py:10
  180.1 10.9 %collective-permute-start = (bf16[64,1152]{1,0:T(8,128)(2,1)S(1)}, bf16[64,1152]{1,0:T(8,128)(2,1)S(1)}, u32[]{:S(2)}, u32[]{:S(2)}) collective-permute-start(bf16[64,1152]{1,0:T(8,128)(2,1)S(1)} %copy.12), channel_id=1, source_target_pairs={{0,1},{1,2},{2,3},{3,4},{4,5},{5,6},{6,7},{7,8},{8,9},{9,10},{10,1... | collective-permute-start | bytes 442376 | tf_op jit(solution)/shard_map/while/body/eval_jaxpr/ppermute | solution.py:10
  185.6 10.4 %collective-permute-start.1 = (f32[64,1152]{1,0:T(8,128)S(1)}, f32[64,1152]{1,0:T(8,128)S(1)}, u32[]{:S(2)}, u32[]{:S(2)}) collective-permute-start(f32[64,1152]{1,0:T(8,128)S(1)} %fusion.49), channel_id=1, source_target_pairs={{0,1},{1,2},{2,3},{3,4},{4,5},{5,6},{6,7},{7,8},{8,9},{9,10},{10,1... | collective-permute-start | bytes 884744 | tf_op jit(solution)/shard_map/while/body/eval_jaxpr/ppermute | solution.py:10
  196.1 10.9 %collective-permute-start = (bf16[64,1152]{1,0:T(8,128)(2,1)S(1)}, bf16[64,1152]{1,0:T(8,128)(2,1)S(1)}, u32[]{:S(2)}, u32[]{:S(2)}) collective-permute-start(bf16[64,1152]{1,0:T(8,128)(2,1)S(1)} %copy.12), channel_id=1, source_target_pairs={{0,1},{1,2},{2,3},{3,4},{4,5},{5,6},{6,7},{7,8},{8,9},{9,10},{10,1... | collective-permute-start | bytes 442376 | tf_op jit(solution)/shard_map/while/body/eval_jaxpr/ppermute | solution.py:10
  201.6 10.4 %collective-permute-start.1 = (f32[64,1152]{1,0:T(8,128)S(1)}, f32[64,1152]{1,0:T(8,128)S(1)}, u32[]{:S(2)}, u32[]{:S(2)}) collective-permute-start(f32[64,1152]{1,0:T(8,128)S(1)} %fusion.49), channel_id=1, source_target_pairs={{0,1},{1,2},{2,3},{3,4},{4,5},{5,6},{6,7},{7,8},{8,9},{9,10},{10,1... | collective-permute-start | bytes 884744 | tf_op jit(solution)/shard_map/while/body/eval_jaxpr/ppermute | solution.py:10
  212.0 10.9 %collective-permute-start = (bf16[64,1152]{1,0:T(8,128)(2,1)S(1)}, bf16[64,1152]{1,0:T(8,128)(2,1)S(1)}, u32[]{:S(2)}, u32[]{:S(2)}) collective-permute-start(bf16[64,1152]{1,0:T(8,128)(2,1)S(1)} %copy.12), channel_id=1, source_target_pairs={{0,1},{1,2},{2,3},{3,4},{4,5},{5,6},{6,7},{7,8},{8,9},{9,10},{10,1... | collective-permute-start | bytes 442376 | tf_op jit(solution)/shard_map/while/body/eval_jaxpr/ppermute | solution.py:10
  217.5 10.4 %collective-permute-start.1 = (f32[64,1152]{1,0:T(8,128)S(1)}, f32[64,1152]{1,0:T(8,128)S(1)}, u32[]{:S(2)}, u32[]{:S(2)}) collective-permute-start(f32[64,1152]{1,0:T(8,128)S(1)} %fusion.49), channel_id=1, source_target_pairs={{0,1},{1,2},{2,3},{3,4},{4,5},{5,6},{6,7},{7,8},{8,9},{9,10},{10,1... | collective-permute-start | bytes 884744 | tf_op jit(solution)/shard_map/while/body/eval_jaxpr/ppermute | solution.py:10
  227.9 10.9 %collective-permute-start = (bf16[64,1152]{1,0:T(8,128)(2,1)S(1)}, bf16[64,1152]{1,0:T(8,128)(2,1)S(1)}, u32[]{:S(2)}, u32[]{:S(2)}) collective-permute-start(bf16[64,1152]{1,0:T(8,128)(2,1)S(1)} %copy.12), channel_id=1, source_target_pairs={{0,1},{1,2},{2,3},{3,4},{4,5},{5,6},{6,7},{7,8},{8,9},{9,10},{10,1... | collective-permute-start | bytes 442376 | tf_op jit(solution)/shard_map/while/body/eval_jaxpr/ppermute | solution.py:10
  233.4 10.4 %collective-permute-start.1 = (f32[64,1152]{1,0:T(8,128)S(1)}, f32[64,1152]{1,0:T(8,128)S(1)}, u32[]{:S(2)}, u32[]{:S(2)}) collective-permute-start(f32[64,1152]{1,0:T(8,128)S(1)} %fusion.49), channel_id=1, source_target_pairs={{0,1},{1,2},{2,3},{3,4},{4,5},{5,6},{6,7},{7,8},{8,9},{9,10},{10,1... | collective-permute-start | bytes 884744 | tf_op jit(solution)/shard_map/while/body/eval_jaxpr/ppermute | solution.py:10
  243.9 10.9 %collective-permute-start = (bf16[64,1152]{1,0:T(8,128)(2,1)S(1)}, bf16[64,1152]{1,0:T(8,128)(2,1)S(1)}, u32[]{:S(2)}, u32[]{:S(2)}) collective-permute-start(bf16[64,1152]{1,0:T(8,128)(2,1)S(1)} %copy.12), channel_id=1, source_target_pairs={{0,1},{1,2},{2,3},{3,4},{4,5},{5,6},{6,7},{7,8},{8,9},{9,10},{10,1... | collective-permute-start | bytes 442376 | tf_op jit(solution)/shard_map/while/body/eval_jaxpr/ppermute | solution.py:10
  249.4 10.4 %collective-permute-start.1 = (f32[64,1152]{1,0:T(8,128)S(1)}, f32[64,1152]{1,0:T(8,128)S(1)}, u32[]{:S(2)}, u32[]{:S(2)}) collective-permute-start(f32[64,1152]{1,0:T(8,128)S(1)} %fusion.49), channel_id=1, source_target_pairs={{0,1},{1,2},{2,3},{3,4},{4,5},{5,6},{6,7},{7,8},{8,9},{9,10},{10,1... | collective-permute-start | bytes 884744 | tf_op jit(solution)/shard_map/while/body/eval_jaxpr/ppermute | solution.py:10
  259.8 10.9 %collective-permute-start = (bf16[64,1152]{1,0:T(8,128)(2,1)S(1)}, bf16[64,1152]{1,0:T(8,128)(2,1)S(1)}, u32[]{:S(2)}, u32[]{:S(2)}) collective-permute-start(bf16[64,1152]{1,0:T(8,128)(2,1)S(1)} %copy.12), channel_id=1, source_target_pairs={{0,1},{1,2},{2,3},{3,4},{4,5},{5,6},{6,7},{7,8},{8,9},{9,10},{10,1... | collective-permute-start | bytes 442376 | tf_op jit(solution)/shard_map/while/body/eval_jaxpr/ppermute | solution.py:10
  265.3 10.4 %collective-permute-start.1 = (f32[64,1152]{1,0:T(8,128)S(1)}, f32[64,1152]{1,0:T(8,128)S(1)}, u32[]{:S(2)}, u32[]{:S(2)}) collective-permute-start(f32[64,1152]{1,0:T(8,128)S(1)} %fusion.49), channel_id=1, source_target_pairs={{0,1},{1,2},{2,3},{3,4},{4,5},{5,6},{6,7},{7,8},{8,9},{9,10},{10,1... | collective-permute-start | bytes 884744 | tf_op jit(solution)/shard_map/while/body/eval_jaxpr/ppermute | solution.py:10
  275.8 10.9 %collective-permute-start = (bf16[64,1152]{1,0:T(8,128)(2,1)S(1)}, bf16[64,1152]{1,0:T(8,128)(2,1)S(1)}, u32[]{:S(2)}, u32[]{:S(2)}) collective-permute-start(bf16[64,1152]{1,0:T(8,128)(2,1)S(1)} %copy.12), channel_id=1, source_target_pairs={{0,1},{1,2},{2,3},{3,4},{4,5},{5,6},{6,7},{7,8},{8,9},{9,10},{10,1... | collective-permute-start | bytes 442376 | tf_op jit(solution)/shard_map/while/body/eval_jaxpr/ppermute | solution.py:10
  281.3 10.4 %collective-permute-start.1 = (f32[64,1152]{1,0:T(8,128)S(1)}, f32[64,1152]{1,0:T(8,128)S(1)}, u32[]{:S(2)}, u32[]{:S(2)}) collective-permute-start(f32[64,1152]{1,0:T(8,128)S(1)} %fusion.49), channel_id=1, source_target_pairs={{0,1},{1,2},{2,3},{3,4},{4,5},{5,6},{6,7},{7,8},{8,9},{9,10},{10,1... | collective-permute-start | bytes 884744 | tf_op jit(solution)/shard_map/while/body/eval_jaxpr/ppermute | solution.py:10
  291.7 10.9 %collective-permute-start = (bf16[64,1152]{1,0:T(8,128)(2,1)S(1)}, bf16[64,1152]{1,0:T(8,128)(2,1)S(1)}, u32[]{:S(2)}, u32[]{:S(2)}) collective-permute-start(bf16[64,1152]{1,0:T(8,128)(2,1)S(1)} %copy.12), channel_id=1, source_target_pairs={{0,1},{1,2},{2,3},{3,4},{4,5},{5,6},{6,7},{7,8},{8,9},{9,10},{10,1... | collective-permute-start | bytes 442376 | tf_op jit(solution)/shard_map/while/body/eval_jaxpr/ppermute | solution.py:10
  297.2 10.4 %collective-permute-start.1 = (f32[64,1152]{1,0:T(8,128)S(1)}, f32[64,1152]{1,0:T(8,128)S(1)}, u32[]{:S(2)}, u32[]{:S(2)}) collective-permute-start(f32[64,1152]{1,0:T(8,128)S(1)} %fusion.49), channel_id=1, source_target_pairs={{0,1},{1,2},{2,3},{3,4},{4,5},{5,6},{6,7},{7,8},{8,9},{9,10},{10,1... | collective-permute-start | bytes 884744 | tf_op jit(solution)/shard_map/while/body/eval_jaxpr/ppermute | solution.py:10
  (4 other events, 85.8 us)
Sparse Core Ops, SparseCore 0:
  10.4 41.1 all-gather.1
  307.8 65.5 reduce-scatter.1
where the time goes:
time: 388 us; the launch traced here: 383 us
  waiting for transfers between devices  184 us (47%)
  matrix products  168 us (43%)
  between operations  14.8 us (4%)
  other arithmetic  8.8 us (2%)
  starting transfers between devices  5.3 us (1%)
    dot_general x16, matrix products, pair_tile(): jnp.dot(weight, text_block, preferred_element_type=jnp.float32)  82.2 us
    ppermute x32, waiting for transfers between devices, from_behind(): return lax.ppermute(value, axis, pairs)  81.5 us
    reduce_scatter x1, waiting for transfers between devices, per_device(): lax.psum_scatter(image_acc, 'grp', scatter_dimension=0, tiled=True)  63.8 us
    dot_general x16, matrix products, pair_tile(): lax.dot_general(images, text_block, (((1,), (1,)), ((), ())), preferred_e...  50.9 us
    all_gather x1, waiting for transfers between devices, per_device(): images = lax.all_gather(image_half, 'grp', axis=0, tiled=True)  38.8 us
    dot_general x16, matrix products, pair_tile(): lax.dot_general(weight, images, (((0,), (0,)), ((), ())), preferred_eleme...  35.2 us
  transfers between devices with their start and end apart: 34, of which 18 were waited for; matrix products, arithmetic and copies ran while one was open for 45% of the time, Pallas kernels for 0%

commit v1 on v0

v1 whole, which is shorter than its diff:
```python
import functools

import jax
import jax.numpy as jnp
from jax import lax
from jax.experimental import pallas as pl
from jax.experimental.pallas import tpu as pltpu
from jax.sharding import PartitionSpec as P

NX, NY, NZ = 4, 4, 8
ROWS = 64
HALF = 32
QUARTER = 16
WIDTH = 1152
GROUP = 256
PLACE = {0: 0, 1: 1, 7: 2, 2: 3, 6: 4, 3: 5, 5: 6, 4: 7}


def coords():
    grp, blk = lax.axis_index("grp"), lax.axis_index("blk")
    core = lax.rem(grp, 2)
    y = lax.rem(grp // 2, NY)
    x = (blk // NZ) * 2 + grp // 8
    return x, y, lax.rem(blk, NZ), core


def device(x, y, z, core):
    x, y, z = lax.rem(x + NX, NX), lax.rem(y + NY, NY), lax.rem(z + NZ, NZ)
    return (lax.rem(x, 2) * 8 + y * 2 + core, (x // 2) * NZ + z)


def normalize(raw):
    values = raw.astype(jnp.float32)
    inverse = lax.rsqrt(jnp.sum(values * values, axis=-1, keepdims=True) + 1e-06)
    return values * inverse, inverse


def tangent(back, unit, inverse):
    along = jnp.sum(unit * back, axis=-1, keepdims=True)
    return ((back - unit * along) * inverse).astype(jnp.bfloat16)


def row_a(dy, dx):
    return dy * GROUP + dx * HALF


def row_b(dx, dy):
    return dx * GROUP + 128 + dy * HALF


def row_i(slot, other=0):
    return PLACE[slot] * 128 + other * ROWS


def kernel(image_ref, text_ref, scale_ref, bias_ref, out_image, out_text,
           images, texts, weight, text_sum, image_sum, text_send, pass_send, image_send, landing,
           send_sem, recv_sem):
    x, y, z, core = coords()
    near = {
        "x+": device(x + 1, y, z, core), "x-": device(x - 1, y, z, core),
        "y+": device(x, y + 1, z, core), "y-": device(x, y - 1, z, core),
        "z+": device(x, y, z + 1, core), "z-": device(x, y, z - 1, core),
        "c": device(x, y, z, 1 - core),
    }
    barrier = pltpu.get_barrier_semaphore()
    for target in near.values():
        pl.semaphore_signal(barrier, inc=1, device_id=target, device_id_type=pl.DeviceIdType.MESH)

    image_unit, _ = normalize(image_ref[...])
    images[pl.ds(0, ROWS), :] = image_unit.astype(jnp.bfloat16)
    text_unit, _ = normalize(text_ref[...])
    text_half = text_unit.astype(jnp.bfloat16)
    texts[pl.ds(row_a(0, 0), HALF), :] = text_half[:HALF]
    texts[pl.ds(row_b(0, 0), HALF), :] = text_half[HALF:]

    pl.semaphore_wait(barrier, len(near))

    copies = {}
    used = [0]

    def send(name, way, src, src_row, dst, dst_row, rows):
        number = len(copies)
        copy = pltpu.make_async_remote_copy(
            src_ref=src.at[pl.ds(src_row, rows)], dst_ref=dst.at[pl.ds(dst_row, rows)],
            send_sem=send_sem.at[number], recv_sem=recv_sem.at[number],
            device_id=near[way], device_id_type=pl.DeviceIdType.MESH,
        )
        copy.start()
        copies[name] = copy

    def arrived(name):
        copies[name].wait_recv()

    def text_hop(name, way, src, dst, rows=HALF):
        send(name, way, texts, src, texts, dst, rows)

    text_hop("ax1", "x+", row_a(0, 0), row_a(0, 1))
    text_hop("by1", "y+", row_b(0, 0), row_b(0, 1))
    text_hop("ax3", "x-", row_a(0, 0), row_a(0, 3))
    text_hop("by3", "y-", row_b(0, 0), row_b(0, 3))

    def image_hop(way, src, dst, part):
        send(f"i{dst}{part}", way, images, row_i(src) + part * HALF, images, row_i(dst) + part * HALF, HALF)

    def image_pass(slot):
        send(f"p{slot}", "c", images, row_i(slot), images, row_i(slot, 1), ROWS)

    for part in (0, 1):
        image_hop("z+", 0, 1, part)
        image_hop("z-", 0, 7, part)
    image_pass(0)

    def spread(k):
        text_hop(f"a1{k}", "y+", row_a(0, k), row_a(1, k))
        text_hop(f"b1{k}", "x+", row_b(0, k), row_b(1, k))
        text_hop(f"a3{k}", "y-", row_a(0, k), row_a(3, k))
        text_hop(f"b3{k}", "x-", row_b(0, k), row_b(3, k))

    spread(0)

    scale_row = jnp.exp(jnp.full((1, GROUP), scale_ref[0], jnp.float32))
    bias_row = jnp.full((1, GROUP), bias_ref[0], jnp.float32)

    def score(group, first, rows):
        block = texts[pl.ds(group * GROUP, GROUP), :]
        logits = lax.dot_general(
            images[pl.ds(first, rows), :], block, (((1,), (1,)), ((), ())), preferred_element_type=jnp.float32
        )
        value = 1.0 / (1.0 + jnp.exp(-(scale_row * logits + bias_row)))
        if group == 0 and first == 0:
            r = lax.broadcasted_iota(jnp.int32, logits.shape, 0)
            c = lax.broadcasted_iota(jnp.int32, logits.shape, 1)
            same = ((r < HALF) & (c == r)) | ((r >= HALF) & (r < ROWS) & (c == r + (128 - HALF)))
            value = value - same.astype(jnp.float32)
        weight[pl.ds(first, rows), pl.ds(group * GROUP, GROUP)] = value.astype(jnp.bfloat16)

    for name in ("ax1", "by1", "ax3", "by3"):
        arrived(name)
    text_hop("ax2p", "x+", row_a(0, 1), row_a(0, 2), QUARTER)
    text_hop("by2p", "y+", row_b(0, 1), row_b(0, 2), QUARTER)
    text_hop("ax2m", "x-", row_a(0, 3) + QUARTER, row_a(0, 2) + QUARTER, QUARTER)
    text_hop("by2m", "y-", row_b(0, 3) + QUARTER, row_b(0, 2) + QUARTER, QUARTER)
    spread(1)
    spread(3)
    for part in (0, 1):
        arrived(f"i1{part}")
        image_hop("z+", 1, 2, part)
        arrived(f"i7{part}")
        image_hop("z-", 7, 6, part)
    image_pass(1)
    image_pass(7)
    for name in ("a10", "b10", "a30", "b30"):
        arrived(name)
    text_hop("a20", "y+", row_a(1, 0), row_a(2, 0))
    text_hop("b20", "x+", row_b(1, 0), row_b(2, 0))
    for name in ("ax2p", "by2p", "ax2m", "by2m"):
        arrived(name)
    spread(2)
    for slot in (0, 1, 7):
        arrived(f"p{slot}")
    score(0, 0, 384)
    for part in (0, 1):
        arrived(f"i2{part}")
        image_hop("z+", 2, 3, part)
        arrived(f"i6{part}")
        image_hop("z-", 6, 5, part)
    image_pass(2)
    image_pass(6)
    for name in ("a11", "b11", "a31", "b31"):
        arrived(name)
    text_hop("a21", "y+", row_a(1, 1), row_a(2, 1))
    text_hop("b21", "x+", row_b(1, 1), row_b(2, 1))
    for name in ("a13", "b13", "a33", "b33"):
        arrived(name)
    text_hop("a23", "y-", row_a(3, 3), row_a(2, 3))
    text_hop("b23", "x-", row_b(3, 3), row_b(2, 3))
    for slot in (2, 6):
        arrived(f"p{slot}")
    score(0, 384, 256)
    for part in (0, 1):
        arrived(f"i3{part}")
        if part == 0:
            image_hop("z+", 3, 4, 0)
        arrived(f"i5{part}")
        if part == 1:
            image_hop("z-", 5, 4, 1)
    image_pass(3)
    image_pass(5)
    for name in ("a12", "b12", "a32", "b32"):
        arrived(name)
    text_hop("a22", "y-", row_a(3, 2), row_a(2, 2))
    text_hop("b22", "x-", row_b(3, 2), row_b(2, 2))
    for slot in (3, 5):
        arrived(f"p{slot}")
    score(0, 640, 256)
    score(1, 0, 896)
    score(3, 0, 896)
    arrived("i40")
    arrived("i41")
    image_pass(4)
    arrived("p4")
    for group in (0, 1, 3):
        score(group, 896, 128)
    for name in ("a20", "b20", "a21", "b21", "a23", "b23", "a22", "b22"):
        arrived(name)
    score(2, 0, 1024)

    landed = {}

    def scatter(name, way, src, src_row, rows):
        landed[name] = used[0]
        send(name, way, src, src_row, landing, used[0], rows)
        used[0] += rows

    def landing_of(name, rows, skip=0):
        return landing[pl.ds(landed[name] + skip, rows), :].astype(jnp.float32)

    def text_back(group):
        columns = pl.ds(group * GROUP, GROUP)
        return lax.dot_general(
            weight[:, columns], images[...], (((0,), (0,)), ((), ())), preferred_element_type=jnp.float32
        )

    def image_back(pair):
        return jnp.dot(
            weight[pl.ds(pair * GROUP, GROUP), :], texts[...], preferred_element_type=jnp.float32
        )

    def image_pair(pair, slots):
        back = image_back(pair)
        for n, slot in enumerate(slots):
            image_sum[pl.ds(pair * 128 + n * ROWS, ROWS), :] = back[n * 128:n * 128 + ROWS]
            pass_send[pl.ds(pair * 128 + n * ROWS, ROWS), :] = back[n * 128 + ROWS:(n + 1) * 128].astype(jnp.bfloat16)
            scatter(f"q{slot}", "c", pass_send, pair * 128 + n * ROWS, ROWS)

    def image_total(slot, skip=0, rows=ROWS):
        return image_sum[pl.ds(PLACE[slot] * ROWS + skip, rows), :] + landing_of(f"q{slot}", rows, skip)

    def image_on(slot, way, total):
        image_send[pl.ds(PLACE[slot] * ROWS, ROWS), :] = total.astype(jnp.bfloat16)
        scatter(f"j{slot}", way, image_send, PLACE[slot] * ROWS, ROWS)

    def text_on(name, way, row, total, skip=0, rows=HALF):
        text_send[pl.ds(row + skip, rows), :] = total.astype(jnp.bfloat16)
        scatter(name, way, text_send, row + skip, rows)

    text_send[pl.ds(2 * GROUP, GROUP), :] = text_back(2).astype(jnp.bfloat16)
    for k, way in ((2, "+"), (0, "-"), (3, "+"), (1, "-")):
        scatter(f"ta2{k}", "y" + way, text_send, row_a(2, k), HALF)
        scatter(f"tb2{k}", "x" + way, text_send, row_b(2, k), HALF)

    image_pair(3, (5, 4))
    arrived("q4")
    total = image_total(4)
    image_send[pl.ds(PLACE[4] * ROWS, ROWS), :] = total.astype(jnp.bfloat16)
    scatter("j4a", "z-", image_send, PLACE[4] * ROWS, HALF)
    scatter("j4b", "z+", image_send, PLACE[4] * ROWS + HALF, HALF)

    text_sum[pl.ds(1 * GROUP, GROUP), :] = text_back(1)
    for k in (2, 3):
        text_on(f"ta1{k}", "y-", row_a(1, k), text_sum[pl.ds(row_a(1, k), HALF), :])
        text_on(f"tb1{k}", "x-", row_b(1, k), text_sum[pl.ds(row_b(1, k), HALF), :])
    text_sum[pl.ds(3 * GROUP, GROUP), :] = text_back(3)
    for k in (1, 0):
        text_on(f"ta3{k}", "y+", row_a(3, k), text_sum[pl.ds(row_a(3, k), HALF), :])
        text_on(f"tb3{k}", "x+", row_b(3, k), text_sum[pl.ds(row_b(3, k), HALF), :])

    image_pair(2, (6, 3))
    arrived("q5")
    arrived("j4b")
    image_send[pl.ds(PLACE[5] * ROWS, HALF), :] = image_total(5, 0, HALF).astype(jnp.bfloat16)
    image_send[pl.ds(PLACE[5] * ROWS + HALF, HALF), :] = (
        image_total(5, HALF, HALF) + landing_of("j4b", HALF)
    ).astype(jnp.bfloat16)
    scatter("j5", "z+", image_send, PLACE[5] * ROWS, ROWS)
    arrived("q3")
    arrived("j4a")
    image_send[pl.ds(PLACE[3] * ROWS, HALF), :] = (
        image_total(3, 0, HALF) + landing_of("j4a", HALF)
    ).astype(jnp.bfloat16)
    image_send[pl.ds(PLACE[3] * ROWS + HALF, HALF), :] = image_total(3, HALF, HALF).astype(jnp.bfloat16)
    scatter("j3", "z-", image_send, PLACE[3] * ROWS, ROWS)

    for k, group, way in ((2, 3, "+"), (0, 1, "-"), (3, 3, "+"), (1, 1, "-")):
        arrived(f"ta2{k}")
        arrived(f"tb2{k}")
        text_on(f"ta{group}{k}", "y" + way, row_a(group, k),
                text_sum[pl.ds(row_a(group, k), HALF), :] + landing_of(f"ta2{k}", HALF))
        text_on(f"tb{group}{k}", "x" + way, row_b(group, k),
                text_sum[pl.ds(row_b(group, k), HALF), :] + landing_of(f"tb2{k}", HALF))

    image_pair(1, (7, 2))
    arrived("q6")
    arrived("j5")
    image_on(6, "z+", image_total(6) + landing_of("j5", ROWS))
    arrived("q2")
    arrived("j3")
    image_on(2, "z-", image_total(2) + landing_of("j3", ROWS))

    text_sum[pl.ds(0, GROUP), :] = text_back(0)

    def reduced(kind, k):
        arrived(f"t{kind}1{k}")
        arrived(f"t{kind}3{k}")
        row = (row_a if kind == "a" else row_b)(0, k)
        return (text_sum[pl.ds(row, HALF), :] + landing_of(f"t{kind}1{k}", HALF)) + landing_of(f"t{kind}3{k}", HALF)

    for kind, axis in (("a", "x"), ("b", "y")):
        row = (row_a if kind == "a" else row_b)(0, 2)
        text_send[pl.ds(row, HALF), :] = reduced(kind, 2).astype(jnp.bfloat16)
        scatter(f"u{kind}2m", axis + "-", text_send, row, QUARTER)
        scatter(f"u{kind}2p", axis + "+", text_send, row + QUARTER, QUARTER)

    image_pair(0, (0, 1))
    arrived("q7")
    arrived("j6")
    image_on(7, "z+", image_total(7) + landing_of("j6", ROWS))
    arrived("q1")
    arrived("j2")
    image_on(1, "z-", image_total(1) + landing_of("j2", ROWS))

    for k, part, way in ((1, "m", "-"), (3, "p", "+")):
        for kind, axis in (("a", "x"), ("b", "y")):
            row = (row_a if kind == "a" else row_b)(0, k)
            total = reduced(kind, k)
            arrived(f"u{kind}2{part}")
            extra = landing_of(f"u{kind}2{part}", QUARTER)
            if part == "m":
                total = jnp.concatenate([total[:QUARTER] + extra, total[QUARTER:]], axis=0)
            else:
                total = jnp.concatenate([total[:QUARTER], total[QUARTER:] + extra], axis=0)
            text_on(f"u{kind}{k}", axis + way, row, total)

    scale = jnp.exp(jnp.full((1, WIDTH), scale_ref[0], jnp.float32))
    image_unit, image_inv = normalize(image_ref[...])
    arrived("q0")
    arrived("j7")
    arrived("j1")
    back = (image_total(0) + landing_of("j7", ROWS)) + landing_of("j1", ROWS)
    out_image[...] = tangent(scale * back, image_unit, image_inv)

    text_unit, text_inv = normalize(text_ref[...])
    for n, kind in enumerate(("a", "b")):
        back = reduced(kind, 0)
        arrived(f"u{kind}1")
        arrived(f"u{kind}3")
        back = (back + landing_of(f"u{kind}1", HALF)) + landing_of(f"u{kind}3", HALF)
        part = slice(n * HALF, (n + 1) * HALF)
        out_text[pl.ds(n * HALF, HALF), :] = tangent(scale * back, text_unit[part], text_inv[part])

    for copy in copies.values():
        copy.wait_send()


COPIES = 120


def per_device(image_raw, text_raw, log_scale, bias):
    block = jax.ShapeDtypeStruct((ROWS, WIDTH), jnp.bfloat16)
    vmem = pl.BlockSpec(memory_space=pltpu.VMEM)
    smem = pl.BlockSpec(memory_space=pltpu.SMEM)
    half, full = jnp.bfloat16, jnp.float32
    return pl.pallas_call(
        kernel,
        out_shape=(block, block),
        in_specs=[vmem, vmem, smem, smem],
        out_specs=(vmem, vmem),
        scratch_shapes=[
            pltpu.VMEM((1024, WIDTH), half),
            pltpu.VMEM((1024, WIDTH), half),
            pltpu.VMEM((1024, 1024), half),
            pltpu.VMEM((1024, WIDTH), full),
            pltpu.VMEM((512, WIDTH), full),
            pltpu.VMEM((1024, WIDTH), half),
            pltpu.VMEM((512, WIDTH), half),
            pltpu.VMEM((512, WIDTH), half),
            pltpu.VMEM((2048, WIDTH), half),
            pltpu.SemaphoreType.DMA((COPIES,)),
            pltpu.SemaphoreType.DMA((COPIES,)),
        ],
        compiler_params=pltpu.CompilerParams(
            collective_id=0, has_side_effects=True, vmem_limit_bytes=52 * 2**20
        ),
        cost_estimate=pl.CostEstimate(flops=7_300_000_000, bytes_accessed=600_000, transcendentals=1_100_000),
    )(image_raw, text_raw, log_scale, bias)


def solution(mesh):
    rows = P(("grp", "blk"), None)
    return jax.shard_map(
        per_device, mesh=mesh, in_specs=(rows, rows, P(), P()), out_specs=(rows, rows), check_vma=False
    )
```

time: 388 us -> 60.8 us (0.16); the launches traced: 383 us -> 60.7 us
  waiting for transfers between devices: 184 us -> 0 us
  matrix products: 168 us -> 0 us
  Pallas kernels: 0 us -> 55.6 us
  between operations: 14.8 us -> 1.94 us
  other arithmetic: 8.8 us -> 0 us
  starting transfers between devices: 5.3 us -> 0 us
    dot_general x48 -> x0, matrix products: 168 us -> none  [the longest x16 82.2 us: pair_tile(): jnp.dot(weight, text_block, preferred_element_type=jnp.float32)]
    ppermute x32 -> x0, waiting for transfers between devices: 81.5 us -> none  [from_behind(): return lax.ppermute(value, axis, pairs)]
    reduce_scatter x1 -> x0, waiting for transfers between devices: 63.8 us -> none  [per_device(): lax.psum_scatter(image_acc, 'grp', scatter_dimension=0, tiled=True)]
    pallas_call x0 -> x1, Pallas kernels: none -> 55.6 us  [per_device(): pl.pallas_call(kernel, out_shape=(block, block), in_specs=[vmem, vmem, sm...]
    all_gather x1 -> x0, waiting for transfers between devices: 38.8 us -> none  [per_device(): images = lax.all_gather(image_half, 'grp', axis=0, tiled=True)]
    convert_element_type x4 -> x0, other arithmetic: 5.23 us -> none  [the longest x2 2.54 us: tangent(): return ((back - unit * along) * inverse).astype(jnp.bfloat16)]
    ppermute x32 -> x0, starting transfers between devices: 5.22 us -> none  [from_behind(): return lax.ppermute(value, axis, pairs)]
  transfers between devices with their start and end apart: 34 -> 0, of which waited for: 18 -> 0; matrix products, arithmetic and copies ran while one was open for 45% -> 0% of each run, Pallas kernels for 0% -> 0%
where the time goes in v1:
time: 60.8 us; the launch traced here: 60.7 us
  Pallas kernels  55.6 us (91%)
  local copies, waits for them, and re-layouts  3.14 us (5%)
  between operations  1.94 us (3%)
    pallas_call x1, Pallas kernels, per_device(): pl.pallas_call(kernel, out_shape=(block, block), in_specs=[vmem, vmem, sm...  55.6 us
    unnamed x6, local copies, waits for them, and re-layouts  3.14 us

profile of v1, /device:TPU:1, one launch (start us, length us, event | category | flops | bytes accessed | tf_op | source)
XLA Modules:
  0.0 60.7 jit_solution(13960010085348697070)
XLA Ops:
  1.9 0.0 copy-start
  1.9 0.9 %copy-done = bf16[64,1152]{1,0:T(8,128)(2,1)S(1)} copy-done((bf16[64,1152]{1,0:T(8,128)(2,1)S(1)}, bf16[64,1152]{1,0:T(8,128)(2,1)}, u32[]{:S(2)}) %copy-start) | copy-done | bytes 147480
  2.8 0.0 copy-start.1
  2.8 0.9 %copy-done.1 = bf16[64,1152]{1,0:T(8,128)(2,1)S(1)} copy-done((bf16[64,1152]{1,0:T(8,128)(2,1)S(1)}, bf16[64,1152]{1,0:T(8,128)(2,1)}, u32[]{:S(2)}) %copy-start.1) | copy-done | bytes 147480
  3.7 55.6 %shard_map.59 = (bf16[64,1152]{1,0:T(8,128)(2,1)S(1)}, bf16[64,1152]{1,0:T(8,128)(2,1)S(1)}) custom-call(bf16[64,1152]{1,0:T(8,128)(2,1)S(1)} %copy-done, bf16[64,1152]{1,0:T(8,128)(2,1)S(1)} %copy-done.1, f32[1]{0:T(128)S(6)} %copy.8.scale_ref, f32[1]{0:T(128)S(6)} %copy.9.bias_ref), custom_call_target="tpu_custom_call" | custom-call | flops 7299999744 | bytes 600000 | tf_op jit(solution)/shard_map/pallas_call | solution.py:363
  59.3 0.7 %copy.10 = bf16[64,1152]{1,0:T(8,128)(2,1)} copy(bf16[64,1152]{1,0:T(8,128)(2,1)S(1)} %get-tuple-element.4) | data formatting | bytes 294912
  60.0 0.7 %copy.11 = bf16[64,1152]{1,0:T(8,128)(2,1)} copy(bf16[64,1152]{1,0:T(8,128)(2,1)S(1)} %get-tuple-element.5) | data formatting | bytes 294912
Async XLA Ops:
  1.9 0.9 %copy-start = (bf16[64,1152]{1,0:T(8,128)(2,1)S(1)}, bf16[64,1152]{1,0:T(8,128)(2,1)}, u32[]{:S(2)}) copy-start(bf16[64,1152]{1,0:T(8,128)(2,1)} %image_ref.1) | copy-start | bytes 442372
  2.8 0.9 %copy-start.1 = (bf16[64,1152]{1,0:T(8,128)(2,1)S(1)}, bf16[64,1152]{1,0:T(8,128)(2,1)}, u32[]{:S(2)}) copy-start(bf16[64,1152]{1,0:T(8,128)(2,1)} %text_ref.1) | copy-start | bytes 442372

commit v2 on v1

v2 whole, which is shorter than its diff:
```python
import functools

import jax
import jax.numpy as jnp
from jax import lax
from jax.experimental import pallas as pl
from jax.experimental.pallas import tpu as pltpu
from jax.sharding import PartitionSpec as P

NX, NY, NZ = 4, 4, 8
ROWS = 64
HALF = 32
QUARTER = 16
WIDTH = 1152
GROUP = 256
PLACE = {0: 0, 1: 1, 7: 2, 2: 3, 6: 4, 3: 5, 5: 6, 4: 7}


def coords():
    grp, blk = lax.axis_index("grp"), lax.axis_index("blk")
    core = lax.rem(grp, 2)
    y = lax.rem(grp // 2, NY)
    x = (blk // NZ) * 2 + grp // 8
    return x, y, lax.rem(blk, NZ), core


def device(x, y, z, core):
    x, y, z = lax.rem(x + NX, NX), lax.rem(y + NY, NY), lax.rem(z + NZ, NZ)
    return (lax.rem(x, 2) * 8 + y * 2 + core, (x // 2) * NZ + z)


def normalize(raw):
    values = raw.astype(jnp.float32)
    inverse = lax.rsqrt(jnp.sum(values * values, axis=-1, keepdims=True) + 1e-06)
    return values * inverse, inverse


def tangent(back, unit, inverse):
    along = jnp.sum(unit * back, axis=-1, keepdims=True)
    return ((back - unit * along) * inverse).astype(jnp.bfloat16)


def row_a(dy, dx):
    return dy * GROUP + dx * HALF


def row_b(dx, dy):
    return dx * GROUP + 128 + dy * HALF


def row_i(slot, other=0):
    return PLACE[slot] * 128 + other * ROWS


def kernel(image_hbm, text_hbm, scale_ref, bias_ref, out_image, out_text,
           image_ref, text_ref, images, texts, weight, text_sum, image_sum, text_send, pass_send, image_send, landing,
           load_sem, send_sem, recv_sem):
    loads = [
        pltpu.make_async_copy(image_hbm, image_ref, load_sem.at[0]),
        pltpu.make_async_copy(text_hbm, text_ref, load_sem.at[1]),
    ]
    for load in loads:
        load.start()
    x, y, z, core = coords()
    near = {
        "x+": device(x + 1, y, z, core), "x-": device(x - 1, y, z, core),
        "y+": device(x, y + 1, z, core), "y-": device(x, y - 1, z, core),
        "z+": device(x, y, z + 1, core), "z-": device(x, y, z - 1, core),
        "c": device(x, y, z, 1 - core),
    }
    barrier = pltpu.get_barrier_semaphore()
    for target in near.values():
        pl.semaphore_signal(barrier, inc=1, device_id=target, device_id_type=pl.DeviceIdType.MESH)

    loads[0].wait()
    image_unit, _ = normalize(image_ref[...])
    images[pl.ds(0, ROWS), :] = image_unit.astype(jnp.bfloat16)
    loads[1].wait()
    text_unit, _ = normalize(text_ref[...])
    text_half = text_unit.astype(jnp.bfloat16)
    texts[pl.ds(row_a(0, 0), HALF), :] = text_half[:HALF]
    texts[pl.ds(row_b(0, 0), HALF), :] = text_half[HALF:]

    pl.semaphore_wait(barrier, len(near))

    copies = {}
    used = [0]

    def send(name, way, src, src_row, dst, dst_row, rows):
        number = len(copies)
        copy = pltpu.make_async_remote_copy(
            src_ref=src.at[pl.ds(src_row, rows)], dst_ref=dst.at[pl.ds(dst_row, rows)],
            send_sem=send_sem.at[number], recv_sem=recv_sem.at[number],
            device_id=near[way], device_id_type=pl.DeviceIdType.MESH,
        )
        copy.start()
        copies[name] = copy

    def arrived(*names):
        for name in names:
            copies[name].wait_recv()

    def text_hop(name, way, src, dst, rows=HALF):
        send(name, way, texts, src, texts, dst, rows)

    def first_hop(k, way, part):
        skip = part * QUARTER
        text_hop(f"ax{k}{part}", "x" + way, row_a(0, 0) + skip, row_a(0, k) + skip, QUARTER)
        text_hop(f"by{k}{part}", "y" + way, row_b(0, 0) + skip, row_b(0, k) + skip, QUARTER)

    def image_hop(way, src, dst, part):
        skip = part * QUARTER
        send(f"i{dst}{part}", way, images, row_i(src) + skip, images, row_i(dst) + skip, QUARTER)

    def image_pass(slot):
        send(f"p{slot}", "c", images, row_i(slot), images, row_i(slot, 1), ROWS)

    def image_step(hop, n):
        up, down = n, (n + 2) % 4
        if hop:
            arrived(f"i{hop}{up}", f"i{8 - hop}{down}")
        if hop < 3 or n < 2:
            image_hop("z+", hop, hop + 1, up)
            image_hop("z-", (8 - hop) % 8, 7 - hop, down)

    def spread(k):
        text_hop(f"a1{k}", "y+", row_a(0, k), row_a(1, k))
        text_hop(f"b1{k}", "x+", row_b(0, k), row_b(1, k))
        text_hop(f"a3{k}", "y-", row_a(0, k), row_a(3, k))
        text_hop(f"b3{k}", "x-", row_b(0, k), row_b(3, k))

    def forward(k, way, near_group):
        arrived(f"a{near_group}{k}", f"b{near_group}{k}")
        text_hop(f"a2{k}", "y" + way, row_a(near_group, k), row_a(2, k))
        text_hop(f"b2{k}", "x" + way, row_b(near_group, k), row_b(2, k))

    first_hop(1, "+", 0)
    first_hop(3, "-", 1)
    image_step(0, 0)
    first_hop(1, "+", 1)
    first_hop(3, "-", 0)
    image_step(0, 1)
    image_pass(0)
    spread(0)
    image_step(0, 2)
    image_step(0, 3)

    scale_row = jnp.exp(jnp.full((1, GROUP), scale_ref[0], jnp.float32))
    bias_row = jnp.full((1, GROUP), bias_ref[0], jnp.float32)

    def score(group, first, rows):
        block = texts[pl.ds(group * GROUP, GROUP), :]
        logits = lax.dot_general(
            images[pl.ds(first, rows), :], block, (((1,), (1,)), ((), ())), preferred_element_type=jnp.float32
        )
        value = 1.0 / (1.0 + jnp.exp(-(scale_row * logits + bias_row)))
        if group == 0 and first == 0:
            r = lax.broadcasted_iota(jnp.int32, logits.shape, 0)
            c = lax.broadcasted_iota(jnp.int32, logits.shape, 1)
            same = ((r < HALF) & (c == r)) | ((r >= HALF) & (r < ROWS) & (c == r + (128 - HALF)))
            value = value - same.astype(jnp.float32)
        weight[pl.ds(first, rows), pl.ds(group * GROUP, GROUP)] = value.astype(jnp.bfloat16)

    arrived("ax10", "by10", "ax31", "by31")
    text_hop("ax20", "x+", row_a(0, 1), row_a(0, 2), QUARTER)
    text_hop("by20", "y+", row_b(0, 1), row_b(0, 2), QUARTER)
    text_hop("ax21", "x-", row_a(0, 3) + QUARTER, row_a(0, 2) + QUARTER, QUARTER)
    text_hop("by21", "y-", row_b(0, 3) + QUARTER, row_b(0, 2) + QUARTER, QUARTER)
    image_step(1, 0)
    arrived("ax11", "by11", "ax30", "by30")
    spread(1)
    spread(3)
    image_step(1, 1)
    image_step(1, 2)
    image_step(1, 3)
    image_pass(1)
    image_pass(7)
    arrived("ax20", "by20", "ax21", "by21")
    spread(2)
    forward(0, "+", 1)
    image_step(2, 0)
    image_step(2, 1)
    arrived("p0", "p1", "p7")
    score(0, 0, 384)
    image_step(2, 2)
    forward(1, "+", 1)
    image_step(2, 3)
    image_pass(2)
    image_pass(6)
    image_step(3, 0)
    forward(3, "-", 3)
    image_step(3, 1)
    arrived("p2", "p6")
    score(0, 384, 256)
    forward(2, "-", 3)
    image_step(3, 2)
    image_step(3, 3)
    image_pass(3)
    image_pass(5)
    arrived("a30", "b30", "a31", "b31", "a12", "b12", "a13", "b13")
    score(1, 0, 640)
    arrived("i40", "i41", "i42", "i43")
    image_pass(4)
    score(3, 0, 640)
    arrived("p3", "p5", "p4")
    for group in (0, 1, 3):
        score(group, 640, 384)
    arrived("a20", "b20", "a21", "b21", "a23", "b23", "a22", "b22")
    score(2, 0, 1024)

    landed = {}

    def scatter(name, way, src, src_row, rows):
        landed[name] = used[0]
        send(name, way, src, src_row, landing, used[0], rows)
        used[0] += rows

    def landing_of(name, rows, skip=0):
        return landing[pl.ds(landed[name] + skip, rows), :].astype(jnp.float32)

    def text_back(group):
        columns = pl.ds(group * GROUP, GROUP)
        return lax.dot_general(
            weight[:, columns], images[...], (((0,), (0,)), ((), ())), preferred_element_type=jnp.float32
        )

    def image_back(pair):
        return jnp.dot(
            weight[pl.ds(pair * GROUP, GROUP), :], texts[...], preferred_element_type=jnp.float32
        )

    def image_pair(pair, slots):
        back = image_back(pair)
        for n, slot in enumerate(slots):
            image_sum[pl.ds(pair * 128 + n * ROWS, ROWS), :] = back[n * 128:n * 128 + ROWS]
            pass_send[pl.ds(pair * 128 + n * ROWS, ROWS), :] = back[n * 128 + ROWS:(n + 1) * 128].astype(jnp.bfloat16)
            scatter(f"q{slot}", "c", pass_send, pair * 128 + n * ROWS, ROWS)

    def image_on(slot, way, before, parts):
        for part in parts:
            row = PLACE[slot] * ROWS + part * QUARTER
            total = image_sum[pl.ds(row, QUARTER), :] + landing_of(f"q{slot}", QUARTER, part * QUARTER)
            if before is not None:
                arrived(f"j{before}{part}")
                total = total + landing_of(f"j{before}{part}", QUARTER)
            image_send[pl.ds(row, QUARTER), :] = total.astype(jnp.bfloat16)
            scatter(f"j{slot}{part}", way, image_send, row, QUARTER)

    def text_row(kind, group, k):
        return (row_a if kind == "a" else row_b)(group, k)

    def text_on(group, k, way, before=None):
        for kind, axis in (("a", "y"), ("b", "x")):
            row = text_row(kind, group, k)
            total = text_sum[pl.ds(row, HALF), :]
            if before is not None:
                arrived(f"t{kind}{before}{k}")
                total = total + landing_of(f"t{kind}{before}{k}", HALF)
            text_send[pl.ds(row, HALF), :] = total.astype(jnp.bfloat16)
            scatter(f"t{kind}{group}{k}", axis + way, text_send, row, HALF)

    def reduced(kind, k):
        arrived(f"t{kind}1{k}", f"t{kind}3{k}")
        total = text_sum[pl.ds(text_row(kind, 0, k), HALF), :]
        return (total + landing_of(f"t{kind}1{k}", HALF)) + landing_of(f"t{kind}3{k}", HALF)

    def second_far():
        for kind, axis in (("a", "x"), ("b", "y")):
            row = text_row(kind, 0, 2)
            text_send[pl.ds(row, HALF), :] = reduced(kind, 2).astype(jnp.bfloat16)
            scatter(f"u{kind}2m", axis + "-", text_send, row, QUARTER)
            scatter(f"u{kind}2p", axis + "+", text_send, row + QUARTER, QUARTER)

    def second_near(k, part, way):
        for kind, axis in (("a", "x"), ("b", "y")):
            row = text_row(kind, 0, k)
            total = reduced(kind, k)
            arrived(f"u{kind}2{part}")
            extra = landing_of(f"u{kind}2{part}", QUARTER)
            if part == "m":
                total = jnp.concatenate([total[:QUARTER] + extra, total[QUARTER:]], axis=0)
            else:
                total = jnp.concatenate([total[:QUARTER], total[QUARTER:] + extra], axis=0)
            text_send[pl.ds(row, HALF), :] = total.astype(jnp.bfloat16)
            scatter(f"u{kind}{k}", axis + way, text_send, row, HALF)

    image_pair(3, (5, 4))
    text_send[pl.ds(2 * GROUP, GROUP), :] = text_back(2).astype(jnp.bfloat16)
    for k, way in ((2, "+"), (1, "-"), (3, "+"), (0, "-")):
        scatter(f"ta2{k}", "y" + way, text_send, row_a(2, k), HALF)
        scatter(f"tb2{k}", "x" + way, text_send, row_b(2, k), HALF)
    arrived("q4", "q5")
    image_on(4, "z-", None, (0, 1))
    image_on(4, "z+", None, (2, 3))
    image_on(5, "z+", None, (0, 1))

    image_pair(2, (6, 3))
    text_sum[pl.ds(1 * GROUP, GROUP), :] = text_back(1)
    text_on(1, 2, "-")
    text_on(1, 3, "-")
    arrived("q3")
    image_on(3, "z-", None, (2, 3))
    text_sum[pl.ds(3 * GROUP, GROUP), :] = text_back(3)
    text_on(3, 1, "+")
    image_on(3, "z-", 4, (0, 1))
    image_on(5, "z+", 4, (2, 3))
    text_on(3, 2, "+", 2)
    text_on(1, 1, "-", 2)
    image_pair(1, (7, 2))
    arrived("q6")
    image_on(6, "z+", 5, (0, 1))
    text_on(3, 3, "+", 2)
    text_on(1, 0, "-", 2)
    text_on(3, 0, "+")
    arrived("q2")
    image_on(2, "z-", 3, (2, 3))
    image_on(6, "z+", 5, (2, 3))
    image_on(2, "z-", 3, (0, 1))
    text_sum[pl.ds(0, GROUP), :] = text_back(0)
    second_far()
    image_pair(0, (0, 1))
    arrived("q7")
    image_on(7, "z+", 6, (0, 1))
    arrived("q1")
    image_on(1, "z-", 2, (2, 3))
    image_on(7, "z+", 6, (2, 3))
    image_on(1, "z-", 2, (0, 1))
    second_near(1, "m", "-")
    second_near(3, "p", "+")

    scale = jnp.exp(jnp.full((1, WIDTH), scale_ref[0], jnp.float32))
    image_unit, image_inv = normalize(image_ref[...])
    arrived("q0")
    for part in range(4):
        arrived(f"j7{part}", f"j1{part}")
    up = jnp.concatenate([landing_of("j70", HALF), landing_of("j72", HALF)], axis=0)
    down = jnp.concatenate([landing_of("j10", HALF), landing_of("j12", HALF)], axis=0)
    back = (image_sum[pl.ds(0, ROWS), :] + landing_of("q0", ROWS)) + (up + down)
    out_image[...] = tangent(scale * back, image_unit, image_inv)

    text_unit, text_inv = normalize(text_ref[...])
    for n, kind in enumerate(("a", "b")):
        back = reduced(kind, 0)
        arrived(f"u{kind}1", f"u{kind}3")
        back = (back + landing_of(f"u{kind}1", HALF)) + landing_of(f"u{kind}3", HALF)
        part = slice(n * HALF, (n + 1) * HALF)
        out_text[pl.ds(n * HALF, HALF), :] = tangent(scale * back, text_unit[part], text_inv[part])

    for copy in copies.values():
        copy.wait_send()


COPIES = 144


def per_device(image_raw, text_raw, log_scale, bias):
    block = jax.ShapeDtypeStruct((ROWS, WIDTH), jnp.bfloat16)
    vmem = pl.BlockSpec(memory_space=pltpu.VMEM)
    smem = pl.BlockSpec(memory_space=pltpu.SMEM)
    hbm = pl.BlockSpec(memory_space=pl.ANY)
    half, full = jnp.bfloat16, jnp.float32
    return pl.pallas_call(
        kernel,
        out_shape=(block, block),
        in_specs=[hbm, hbm, smem, smem],
        out_specs=(vmem, vmem),
        scratch_shapes=[
            pltpu.VMEM((ROWS, WIDTH), half),
            pltpu.VMEM((ROWS, WIDTH), half),
            pltpu.VMEM((1024, WIDTH), half),
            pltpu.VMEM((1024, WIDTH), half),
            pltpu.VMEM((1024, 1024), half),
            pltpu.VMEM((1024, WIDTH), full),
            pltpu.VMEM((512, WIDTH), full),
            pltpu.VMEM((1024, WIDTH), half),
            pltpu.VMEM((512, WIDTH), half),
            pltpu.VMEM((512, WIDTH), half),
            pltpu.VMEM((2048, WIDTH), half),
            pltpu.SemaphoreType.DMA((2,)),
            pltpu.SemaphoreType.DMA((COPIES,)),
            pltpu.SemaphoreType.DMA((COPIES,)),
        ],
        compiler_params=pltpu.CompilerParams(
            collective_id=0, has_side_effects=True, vmem_limit_bytes=52 * 2**20
        ),
        cost_estimate=pl.CostEstimate(flops=7_300_000_000, bytes_accessed=600_000, transcendentals=1_100_000),
    )(image_raw, text_raw, log_scale, bias)


def solution(mesh):
    rows = P(("grp", "blk"), None)
    return jax.shard_map(
        per_device, mesh=mesh, in_specs=(rows, rows, P(), P()), out_specs=(rows, rows), check_vma=False
    )
```

time: 60.8 us -> 56.3 us (0.926)
  Pallas kernels: 55.6 us -> 51.1 us
    pallas_call x1, Pallas kernels: 55.6 us -> 51.1 us  [per_device(): pl.pallas_call(kernel, out_shape=(block, block), in_specs=[hbm, hbm, smem...]
where the time goes in v2:
time: 56.3 us; the launch traced here: 56.2 us
  Pallas kernels  51.1 us (91%)
  local copies, waits for them, and re-layouts  3.14 us (6%)
  between operations  1.94 us (3%)
    pallas_call x1, Pallas kernels, per_device(): pl.pallas_call(kernel, out_shape=(block, block), in_specs=[hbm, hbm, smem...  51.1 us
    unnamed x6, local copies, waits for them, and re-layouts  3.14 us

profile of v2, /device:TPU:1, one launch (start us, length us, event | category | flops | bytes accessed | tf_op | source)
XLA Modules:
  0.0 56.2 jit_solution(6462231065526441518)
XLA Ops:
  1.9 0.0 copy-start
  1.9 0.9 %copy-done = bf16[64,1152]{1,0:T(8,128)(2,1)S(1)} copy-done((bf16[64,1152]{1,0:T(8,128)(2,1)S(1)}, bf16[64,1152]{1,0:T(8,128)(2,1)}, u32[]{:S(2)}) %copy-start) | copy-done | bytes 147480
  2.8 0.0 copy-start.1
  2.8 0.9 %copy-done.1 = bf16[64,1152]{1,0:T(8,128)(2,1)S(1)} copy-done((bf16[64,1152]{1,0:T(8,128)(2,1)S(1)}, bf16[64,1152]{1,0:T(8,128)(2,1)}, u32[]{:S(2)}) %copy-start.1) | copy-done | bytes 147480
  3.7 51.1 %shard_map.59 = (bf16[64,1152]{1,0:T(8,128)(2,1)S(1)}, bf16[64,1152]{1,0:T(8,128)(2,1)S(1)}) custom-call(bf16[64,1152]{1,0:T(8,128)(2,1)S(1)} %copy-done, bf16[64,1152]{1,0:T(8,128)(2,1)S(1)} %copy-done.1, f32[1]{0:T(128)S(6)} %copy.8.scale_ref, f32[1]{0:T(128)S(6)} %copy.9.bias_ref), custom_call_target="tpu_custom_call" | custom-call | flops 7299999744 | bytes 600000 | tf_op jit(solution)/shard_map/pallas_call | solution.py:362
  54.9 0.7 %copy.10 = bf16[64,1152]{1,0:T(8,128)(2,1)} copy(bf16[64,1152]{1,0:T(8,128)(2,1)S(1)} %get-tuple-element.4) | data formatting | bytes 294912
  55.5 0.7 %copy.11 = bf16[64,1152]{1,0:T(8,128)(2,1)} copy(bf16[64,1152]{1,0:T(8,128)(2,1)S(1)} %get-tuple-element.5) | data formatting | bytes 294912
Async XLA Ops:
  1.9 0.9 %copy-start = (bf16[64,1152]{1,0:T(8,128)(2,1)S(1)}, bf16[64,1152]{1,0:T(8,128)(2,1)}, u32[]{:S(2)}) copy-start(bf16[64,1152]{1,0:T(8,128)(2,1)} %image_hbm.1) | copy-start | bytes 442372
  2.8 0.9 %copy-start.1 = (bf16[64,1152]{1,0:T(8,128)(2,1)S(1)}, bf16[64,1152]{1,0:T(8,128)(2,1)}, u32[]{:S(2)}) copy-start(bf16[64,1152]{1,0:T(8,128)(2,1)} %text_hbm.1) | copy-start | bytes 442372

commit v3 on v2

--- a/solution.py
+++ b/solution.py
@@ -52,15 +52,9 @@
     return PLACE[slot] * 128 + other * ROWS
 
 
-def kernel(image_hbm, text_hbm, scale_ref, bias_ref, out_image, out_text,
-           image_ref, text_ref, images, texts, weight, text_sum, image_sum, text_send, pass_send, image_send, landing,
-           load_sem, send_sem, recv_sem):
-    loads = [
-        pltpu.make_async_copy(image_hbm, image_ref, load_sem.at[0]),
-        pltpu.make_async_copy(text_hbm, text_ref, load_sem.at[1]),
-    ]
-    for load in loads:
-        load.start()
+def kernel(image_ref, text_ref, scale_ref, bias_ref, out_image, out_text,
+           images, texts, weight, text_sum, image_sum, text_send, pass_send, image_send, landing,
+           send_sem, recv_sem):
     x, y, z, core = coords()
     near = {
         "x+": device(x + 1, y, z, core), "x-": device(x - 1, y, z, core),
@@ -72,14 +66,12 @@
     for target in near.values():
         pl.semaphore_signal(barrier, inc=1, device_id=target, device_id_type=pl.DeviceIdType.MESH)
 
-    loads[0].wait()
-    image_unit, _ = normalize(image_ref[...])
-    images[pl.ds(0, ROWS), :] = image_unit.astype(jnp.bfloat16)
-    loads[1].wait()
     text_unit, _ = normalize(text_ref[...])
     text_half = text_unit.astype(jnp.bfloat16)
     texts[pl.ds(row_a(0, 0), HALF), :] = text_half[:HALF]
     texts[pl.ds(row_b(0, 0), HALF), :] = text_half[HALF:]
+    image_unit, _ = normalize(image_ref[...])
+    images[pl.ds(0, ROWS), :] = image_unit.astype(jnp.bfloat16)
 
     pl.semaphore_wait(barrier, len(near))
 
@@ -145,21 +137,19 @@
     image_step(0, 2)
     image_step(0, 3)
 
-    scale_row = jnp.exp(jnp.full((1, GROUP), scale_ref[0], jnp.float32))
-    bias_row = jnp.full((1, GROUP), bias_ref[0], jnp.float32)
-
-    def score(group, first, rows):
-        block = texts[pl.ds(group * GROUP, GROUP), :]
+    def score(first, rows, column, width):
+        block = texts[pl.ds(column, width), :]
         logits = lax.dot_general(
             images[pl.ds(first, rows), :], block, (((1,), (1,)), ((), ())), preferred_element_type=jnp.float32
         )
-        value = 1.0 / (1.0 + jnp.exp(-(scale_row * logits + bias_row)))
-        if group == 0 and first == 0:
+        scale_row = jnp.exp(jnp.full((1, width), scale_ref[0], jnp.float32))
+        value = 1.0 / (1.0 + jnp.exp(-(scale_row * logits + jnp.full((1, width), bias_ref[0], jnp.float32))))
+        if column == 0 and first == 0:
             r = lax.broadcasted_iota(jnp.int32, logits.shape, 0)
             c = lax.broadcasted_iota(jnp.int32, logits.shape, 1)
             same = ((r < HALF) & (c == r)) | ((r >= HALF) & (r < ROWS) & (c == r + (128 - HALF)))
             value = value - same.astype(jnp.float32)
-        weight[pl.ds(first, rows), pl.ds(group * GROUP, GROUP)] = value.astype(jnp.bfloat16)
+        weight[pl.ds(first, rows), pl.ds(column, width)] = value.astype(jnp.bfloat16)
 
     arrived("ax10", "by10", "ax31", "by31")
     text_hop("ax20", "x+", row_a(0, 1), row_a(0, 2), QUARTER)
@@ -181,7 +171,7 @@
     image_step(2, 0)
     image_step(2, 1)
     arrived("p0", "p1", "p7")
-    score(0, 0, 384)
+    score(0, 384, 0, GROUP)
     image_step(2, 2)
     forward(1, "+", 1)
     image_step(2, 3)
@@ -190,23 +180,23 @@
     image_step(3, 0)
     forward(3, "-", 3)
     image_step(3, 1)
-    arrived("p2", "p6")
-    score(0, 384, 256)
     forward(2, "-", 3)
     image_step(3, 2)
     image_step(3, 3)
     image_pass(3)
     image_pass(5)
+    arrived("p2", "p6")
+    score(384, 256, 0, GROUP)
     arrived("a30", "b30", "a31", "b31", "a12", "b12", "a13", "b13")
-    score(1, 0, 640)
+    score(0, 640, GROUP, GROUP)
     arrived("i40", "i41", "i42", "i43")
     image_pass(4)
-    score(3, 0, 640)
-    arrived("p3", "p5", "p4")
-    for group in (0, 1, 3):
-        score(group, 640, 384)
+    score(0, 640, 3 * GROUP, GROUP)
+    arrived("p3", "p5")
+    score(640, 256, 0, 2 * GROUP)
+    score(640, 256, 3 * GROUP, GROUP)
     arrived("a20", "b20", "a21", "b21", "a23", "b23", "a22", "b22")
-    score(2, 0, 1024)
+    score(0, 896, 2 * GROUP, GROUP)
 
     landed = {}
 
@@ -218,23 +208,21 @@
     def landing_of(name, rows, skip=0):
         return landing[pl.ds(landed[name] + skip, rows), :].astype(jnp.float32)
 
-    def text_back(group):
-        columns = pl.ds(group * GROUP, GROUP)
+    def text_back(group, first=0, rows=1024):
         return lax.dot_general(
-            weight[:, columns], images[...], (((0,), (0,)), ((), ())), preferred_element_type=jnp.float32
+            weight[pl.ds(first, rows), pl.ds(group * GROUP, GROUP)], images[pl.ds(first, rows), :],
+            (((0,), (0,)), ((), ())), preferred_element_type=jnp.float32,
         )
 
-    def image_back(pair):
-        return jnp.dot(
-            weight[pl.ds(pair * GROUP, GROUP), :], texts[...], preferred_element_type=jnp.float32
+    def image_back(*slots):
+        back = jnp.dot(
+            weight[pl.ds(row_i(slots[0]), 128 * len(slots)), :], texts[...], preferred_element_type=jnp.float32
         )
-
-    def image_pair(pair, slots):
-        back = image_back(pair)
         for n, slot in enumerate(slots):
-            image_sum[pl.ds(pair * 128 + n * ROWS, ROWS), :] = back[n * 128:n * 128 + ROWS]
-            pass_send[pl.ds(pair * 128 + n * ROWS, ROWS), :] = back[n * 128 + ROWS:(n + 1) * 128].astype(jnp.bfloat16)
-            scatter(f"q{slot}", "c", pass_send, pair * 128 + n * ROWS, ROWS)
+            place = PLACE[slot] * ROWS
+            pass_send[pl.ds(place, ROWS), :] = back[n * 128 + ROWS:(n + 1) * 128].astype(jnp.bfloat16)
+            scatter(f"q{slot}", "c", pass_send, place, ROWS)
+            image_sum[pl.ds(place, ROWS), :] = back[n * 128:n * 128 + ROWS]
 
     def image_on(slot, way, before, parts):
         for part in parts:
@@ -284,49 +272,54 @@
             text_send[pl.ds(row, HALF), :] = total.astype(jnp.bfloat16)
             scatter(f"u{kind}{k}", axis + way, text_send, row, HALF)
 
-    image_pair(3, (5, 4))
-    text_send[pl.ds(2 * GROUP, GROUP), :] = text_back(2).astype(jnp.bfloat16)
-    for k, way in ((2, "+"), (1, "-"), (3, "+"), (0, "-")):
+    def far_on(k, way):
         scatter(f"ta2{k}", "y" + way, text_send, row_a(2, k), HALF)
         scatter(f"tb2{k}", "x" + way, text_send, row_b(2, k), HALF)
-    arrived("q4", "q5")
+
+    arrived("p4")
+    score(896, 128, 0, 4 * GROUP)
+    text_send[pl.ds(2 * GROUP, GROUP), :] = text_back(2).astype(jnp.bfloat16)
+    far_on(2, "+")
+    far_on(1, "-")
+    far_on(3, "+")
+    image_back(4)
+    image_back(3, 5)
+    text_sum[pl.ds(1 * GROUP, GROUP), :] = text_back(1)
+    text_on(1, 2, "-")
+    far_on(0, "-")
+    arrived("q4")
     image_on(4, "z-", None, (0, 1))
     image_on(4, "z+", None, (2, 3))
+    text_sum[pl.ds(3 * GROUP, GROUP), :] = text_back(3)
+    arrived("q3", "q5")
+    image_on(3, "z-", None, (2, 3))
     image_on(5, "z+", None, (0, 1))
-
-    image_pair(2, (6, 3))
-    text_sum[pl.ds(1 * GROUP, GROUP), :] = text_back(1)
-    text_on(1, 2, "-")
+    text_on(3, 2, "+", 2)
+    text_on(3, 1, "+")
+    text_on(1, 1, "-", 2)
     text_on(1, 3, "-")
-    arrived("q3")
-    image_on(3, "z-", None, (2, 3))
-    text_sum[pl.ds(3 * GROUP, GROUP), :] = text_back(3)
-    text_on(3, 1, "+")
+    image_back(2, 6)
     image_on(3, "z-", 4, (0, 1))
     image_on(5, "z+", 4, (2, 3))
-    text_on(3, 2, "+", 2)
-    text_on(1, 1, "-", 2)
-    image_pair(1, (7, 2))
-    arrived("q6")
+    text_on(3, 3, "+", 2)
+    text_sum[pl.ds(0, GROUP), :] = text_back(0)
+    arrived("q2", "q6")
+    image_on(2, "z-", 3, (2, 3))
     image_on(6, "z+", 5, (0, 1))
-    text_on(3, 3, "+", 2)
+    image_back(1, 7)
+    second_far()
+    image_on(2, "z-", 3, (0, 1))
+    image_on(6, "z+", 5, (2, 3))
     text_on(1, 0, "-", 2)
     text_on(3, 0, "+")
-    arrived("q2")
-    image_on(2, "z-", 3, (2, 3))
-    image_on(6, "z+", 5, (2, 3))
-    image_on(2, "z-", 3, (0, 1))
-    text_sum[pl.ds(0, GROUP), :] = text_back(0)
-    second_far()
-    image_pair(0, (0, 1))
-    arrived("q7")
+    image_back(0)
+    arrived("q1", "q7")
+    image_on(1, "z-", 2, (2, 3))
     image_on(7, "z+", 6, (0, 1))
-    arrived("q1")
-    image_on(1, "z-", 2, (2, 3))
-    image_on(7, "z+", 6, (2, 3))
-    image_on(1, "z-", 2, (0, 1))
     second_near(1, "m", "-")
     second_near(3, "p", "+")
+    image_on(1, "z-", 2, (0, 1))
+    image_on(7, "z+", 6, (2, 3))
 
     scale = jnp.exp(jnp.full((1, WIDTH), scale_ref[0], jnp.float32))
     image_unit, image_inv = normalize(image_ref[...])
@@ -357,16 +350,13 @@
     block = jax.ShapeDtypeStruct((ROWS, WIDTH), jnp.bfloat16)
     vmem = pl.BlockSpec(memory_space=pltpu.VMEM)
     smem = pl.BlockSpec(memory_space=pltpu.SMEM)
-    hbm = pl.BlockSpec(memory_space=pl.ANY)
     half, full = jnp.bfloat16, jnp.float32
     return pl.pallas_call(
         kernel,
         out_shape=(block, block),
-        in_specs=[hbm, hbm, smem, smem],
+        in_specs=[vmem, vmem, smem, smem],
         out_specs=(vmem, vmem),
         scratch_shapes=[
-            pltpu.VMEM((ROWS, WIDTH), half),
-            pltpu.VMEM((ROWS, WIDTH), half),
             pltpu.VMEM((1024, WIDTH), half),
             pltpu.VMEM((1024, WIDTH), half),
             pltpu.VMEM((1024, 1024), half),
@@ -376,7 +366,6 @@
             pltpu.VMEM((512, WIDTH), half),
             pltpu.VMEM((512, WIDTH), half),
             pltpu.VMEM((2048, WIDTH), half),
-            pltpu.SemaphoreType.DMA((2,)),
             pltpu.SemaphoreType.DMA((COPIES,)),
             pltpu.SemaphoreType.DMA((COPIES,)),
         ],

time: 56.3 us -> 55.9 us (level)
  no operation moved by 1% of the time
where the time goes in v3:
time: 55.9 us; the launch traced here: 55.8 us
  Pallas kernels  50.7 us (91%)
  local copies, waits for them, and re-layouts  3.14 us (6%)
  between operations  1.94 us (3%)
    pallas_call x1, Pallas kernels, per_device(): pl.pallas_call(kernel, out_shape=(block, block), in_specs=[vmem, vmem, sm...  50.7 us
    unnamed x6, local copies, waits for them, and re-layouts  3.14 us

profile of v3, /device:TPU:1, one launch (start us, length us, event | category | flops | bytes accessed | tf_op | source)
XLA Modules:
  0.0 55.8 jit_solution(3916757056053061515)
XLA Ops:
  1.9 0.0 copy-start
  1.9 0.9 %copy-done = bf16[64,1152]{1,0:T(8,128)(2,1)S(1)} copy-done((bf16[64,1152]{1,0:T(8,128)(2,1)S(1)}, bf16[64,1152]{1,0:T(8,128)(2,1)}, u32[]{:S(2)}) %copy-start) | copy-done | bytes 147480
  2.8 0.0 copy-start.1
  2.8 0.9 %copy-done.1 = bf16[64,1152]{1,0:T(8,128)(2,1)S(1)} copy-done((bf16[64,1152]{1,0:T(8,128)(2,1)S(1)}, bf16[64,1152]{1,0:T(8,128)(2,1)}, u32[]{:S(2)}) %copy-start.1) | copy-done | bytes 147480
  3.7 50.7 %shard_map.59 = (bf16[64,1152]{1,0:T(8,128)(2,1)S(1)}, bf16[64,1152]{1,0:T(8,128)(2,1)S(1)}) custom-call(bf16[64,1152]{1,0:T(8,128)(2,1)S(1)} %copy-done, bf16[64,1152]{1,0:T(8,128)(2,1)S(1)} %copy-done.1, f32[1]{0:T(128)S(6)} %copy.8.scale_ref, f32[1]{0:T(128)S(6)} %copy.9.bias_ref), custom_call_target="tpu_custom_call" | custom-call | flops 7299999744 | bytes 600000 | tf_op jit(solution)/shard_map/pallas_call | solution.py:354
  54.5 0.7 %copy.10 = bf16[64,1152]{1,0:T(8,128)(2,1)} copy(bf16[64,1152]{1,0:T(8,128)(2,1)S(1)} %get-tuple-element.4) | data formatting | bytes 294912
  55.1 0.7 %copy.11 = bf16[64,1152]{1,0:T(8,128)(2,1)} copy(bf16[64,1152]{1,0:T(8,128)(2,1)S(1)} %get-tuple-element.5) | data formatting | bytes 294912
Async XLA Ops:
  1.9 0.9 %copy-start = (bf16[64,1152]{1,0:T(8,128)(2,1)S(1)}, bf16[64,1152]{1,0:T(8,128)(2,1)}, u32[]{:S(2)}) copy-start(bf16[64,1152]{1,0:T(8,128)(2,1)} %image_ref.1) | copy-start | bytes 442372
  2.8 0.9 %copy-start.1 = (bf16[64,1152]{1,0:T(8,128)(2,1)S(1)}, bf16[64,1152]{1,0:T(8,128)(2,1)}, u32[]{:S(2)}) copy-start(bf16[64,1152]{1,0:T(8,128)(2,1)} %text_ref.1) | copy-start | bytes 442372

commit v4 on v3

--- a/solution.py
+++ b/solution.py
@@ -52,9 +52,10 @@
     return PLACE[slot] * 128 + other * ROWS
 
 
-def kernel(image_ref, text_ref, scale_ref, bias_ref, out_image, out_text,
+def kernel(raw_ref, scale_ref, bias_ref, out,
            images, texts, weight, text_sum, image_sum, text_send, pass_send, image_send, landing,
            send_sem, recv_sem):
+    image_ref, text_ref = raw_ref.at[pl.ds(0, ROWS)], raw_ref.at[pl.ds(ROWS, ROWS)]
     x, y, z, core = coords()
     near = {
         "x+": device(x + 1, y, z, core), "x-": device(x - 1, y, z, core),
@@ -329,7 +330,7 @@
     up = jnp.concatenate([landing_of("j70", HALF), landing_of("j72", HALF)], axis=0)
     down = jnp.concatenate([landing_of("j10", HALF), landing_of("j12", HALF)], axis=0)
     back = (image_sum[pl.ds(0, ROWS), :] + landing_of("q0", ROWS)) + (up + down)
-    out_image[...] = tangent(scale * back, image_unit, image_inv)
+    out[pl.ds(0, ROWS), :] = tangent(scale * back, image_unit, image_inv)
 
     text_unit, text_inv = normalize(text_ref[...])
     for n, kind in enumerate(("a", "b")):
@@ -337,7 +338,7 @@
         arrived(f"u{kind}1", f"u{kind}3")
         back = (back + landing_of(f"u{kind}1", HALF)) + landing_of(f"u{kind}3", HALF)
         part = slice(n * HALF, (n + 1) * HALF)
-        out_text[pl.ds(n * HALF, HALF), :] = tangent(scale * back, text_unit[part], text_inv[part])
+        out[pl.ds(ROWS + n * HALF, HALF), :] = tangent(scale * back, text_unit[part], text_inv[part])
 
     for copy in copies.values():
         copy.wait_send()
@@ -347,15 +348,15 @@
 
 
 def per_device(image_raw, text_raw, log_scale, bias):
-    block = jax.ShapeDtypeStruct((ROWS, WIDTH), jnp.bfloat16)
+    block = jax.ShapeDtypeStruct((2 * ROWS, WIDTH), jnp.bfloat16)
     vmem = pl.BlockSpec(memory_space=pltpu.VMEM)
     smem = pl.BlockSpec(memory_space=pltpu.SMEM)
     half, full = jnp.bfloat16, jnp.float32
-    return pl.pallas_call(
+    both = pl.pallas_call(
         kernel,
-        out_shape=(block, block),
-        in_specs=[vmem, vmem, smem, smem],
-        out_specs=(vmem, vmem),
+        out_shape=block,
+        in_specs=[vmem, smem, smem],
+        out_specs=vmem,
         scratch_shapes=[
             pltpu.VMEM((1024, WIDTH), half),
             pltpu.VMEM((1024, WIDTH), half),
@@ -373,7 +374,8 @@
             collective_id=0, has_side_effects=True, vmem_limit_bytes=52 * 2**20
         ),
         cost_estimate=pl.CostEstimate(flops=7_300_000_000, bytes_accessed=600_000, transcendentals=1_100_000),
-    )(image_raw, text_raw, log_scale, bias)
+    )(jnp.concatenate([image_raw, text_raw], axis=0), log_scale, bias)
+    return both[:ROWS], both[ROWS:]
 
 
 def solution(mesh):

time: 55.9 us -> 54.4 us (0.973)
  local copies, waits for them, and re-layouts: 3.14 us -> 0.73 us
  other arithmetic: 0 us -> 1.01 us
    unnamed x6 -> x0, local copies, waits for them, and re-layouts: 3.14 us -> none
    concatenate x0 -> x1, other arithmetic: none -> 1.01 us  [per_device(): jnp.concatenate([image_raw, text_raw], axis=0)]
    slice x0 -> x1, local copies, waits for them, and re-layouts: none -> 0.73 us  [per_device(): return (both[:ROWS], both[ROWS:])]
where the time goes in v4:
time: 54.4 us; the launch traced here: 54.3 us
  Pallas kernels  50.6 us (93%)
  between operations  1.93 us (4%)
  other arithmetic  1.01 us (2%)
  local copies, waits for them, and re-layouts  0.73 us (1%)
    pallas_call x1, Pallas kernels, per_device(): pl.pallas_call(kernel, out_shape=block, in_specs=[vmem, smem, smem], out_...  50.6 us

profile of v4, /device:TPU:1, one launch (start us, length us, event | category | flops | bytes accessed | tf_op | source)
XLA Modules:
  0.0 54.3 jit_solution(4614848750068758784)
XLA Ops:
  1.9 1.0 %pad_maximum_fusion.raw_ref = bf16[128,1152]{1,0:T(8,128)(2,1)S(1)} fusion(bf16[64,1152]{1,0:T(8,128)(2,1)} %param.5, bf16[64,1152]{1,0:T(8,128)(2,1)} %param.4), kind=kLoop, calls=%fused_computation | loop fusion | flops 589824 | bytes 589824 | tf_op jit(solution)/shard_map/concatenate | solution.py:377
  2.9 50.6 %shard_map.59 = bf16[128,1152]{1,0:T(8,128)(2,1)S(1)} custom-call(bf16[128,1152]{1,0:T(8,128)(2,1)S(1)} %pad_maximum_fusion.raw_ref, f32[1]{0:T(128)S(6)} %copy.6.scale_ref, f32[1]{0:T(128)S(6)} %copy.7.bias_ref), custom_call_target="tpu_custom_call" | custom-call | flops 7299999744 | bytes 600000 | tf_op jit(solution)/shard_map/pallas_call | solution.py:355
  53.6 0.7 %fusion = (bf16[64,1152]{1,0:T(8,128)(2,1)}, bf16[64,1152]{1,0:T(8,128)(2,1)}) fusion(bf16[128,1152]{1,0:T(8,128)(2,1)S(1)} %shard_map.59), kind=kLoop, calls=%fused_computation.1 | loop fusion | bytes 589824 | tf_op jit(solution)/shard_map/slice | solution.py:378

commit v5 on v4

--- a/solution.py
+++ b/solution.py
@@ -40,12 +40,18 @@
     return ((back - unit * along) * inverse).astype(jnp.bfloat16)
 
 
+def text_place(group, k):
+    if group in (0, 2):
+        return group // 2 * 3 * GROUP + k * HALF
+    return (GROUP if k < 2 else 2 * GROUP) + group // 2 * ROWS + k % 2 * HALF
+
+
 def row_a(dy, dx):
-    return dy * GROUP + dx * HALF
+    return text_place(dy, dx)
 
 
 def row_b(dx, dy):
-    return dx * GROUP + 128 + dy * HALF
+    return text_place(dx, dy) + 128
 
 
 def row_i(slot, other=0):
@@ -178,6 +184,8 @@
     image_step(2, 3)
     image_pass(2)
     image_pass(6)
+    arrived("a30", "b30", "a31", "b31")
+    score(0, 384, GROUP, GROUP)
     image_step(3, 0)
     forward(3, "-", 3)
     image_step(3, 1)
@@ -187,17 +195,15 @@
     image_pass(3)
     image_pass(5)
     arrived("p2", "p6")
-    score(384, 256, 0, GROUP)
-    arrived("a30", "b30", "a31", "b31", "a12", "b12", "a13", "b13")
-    score(0, 640, GROUP, GROUP)
+    score(384, 256, 0, 2 * GROUP)
+    arrived("a12", "b12", "a13", "b13")
+    score(0, 640, 2 * GROUP, GROUP)
     arrived("i40", "i41", "i42", "i43")
     image_pass(4)
-    score(0, 640, 3 * GROUP, GROUP)
     arrived("p3", "p5")
-    score(640, 256, 0, 2 * GROUP)
-    score(640, 256, 3 * GROUP, GROUP)
+    score(640, 256, 0, 3 * GROUP)
     arrived("a20", "b20", "a21", "b21", "a23", "b23", "a22", "b22")
-    score(0, 896, 2 * GROUP, GROUP)
+    score(0, 896, 3 * GROUP, GROUP)
 
     landed = {}
 
@@ -279,19 +285,19 @@
 
     arrived("p4")
     score(896, 128, 0, 4 * GROUP)
-    text_send[pl.ds(2 * GROUP, GROUP), :] = text_back(2).astype(jnp.bfloat16)
+    text_send[pl.ds(3 * GROUP, GROUP), :] = text_back(3).astype(jnp.bfloat16)
     far_on(2, "+")
     far_on(1, "-")
     far_on(3, "+")
     image_back(4)
     image_back(3, 5)
-    text_sum[pl.ds(1 * GROUP, GROUP), :] = text_back(1)
+    text_sum[pl.ds(2 * GROUP, GROUP), :] = text_back(2)
     text_on(1, 2, "-")
     far_on(0, "-")
     arrived("q4")
     image_on(4, "z-", None, (0, 1))
     image_on(4, "z+", None, (2, 3))
-    text_sum[pl.ds(3 * GROUP, GROUP), :] = text_back(3)
+    text_sum[pl.ds(1 * GROUP, GROUP), :] = text_back(1)
     arrived("q3", "q5")
     image_on(3, "z-", None, (2, 3))
     image_on(5, "z+", None, (0, 1))

time: 54.4 us -> 53 us (0.974)
  Pallas kernels: 50.6 us -> 49.2 us
    pallas_call x1, Pallas kernels: 50.6 us -> 49.2 us  [per_device(): pl.pallas_call(kernel, out_shape=block, in_specs=[vmem, smem, smem], out_...]
where the time goes in v5:
time: 53 us; the launch traced here: 52.9 us
  Pallas kernels  49.2 us (93%)
  between operations  1.93 us (4%)
  other arithmetic  1.01 us (2%)
  local copies, waits for them, and re-layouts  0.73 us (1%)
    pallas_call x1, Pallas kernels, per_device(): pl.pallas_call(kernel, out_shape=block, in_specs=[vmem, smem, smem], out_...  49.2 us

profile of v5, /device:TPU:1, one launch (start us, length us, event | category | flops | bytes accessed | tf_op | source)
XLA Modules:
  0.0 52.9 jit_solution(11447117166094215090)
XLA Ops:
  1.9 1.0 %pad_maximum_fusion.raw_ref = bf16[128,1152]{1,0:T(8,128)(2,1)S(1)} fusion(bf16[64,1152]{1,0:T(8,128)(2,1)} %param.5, bf16[64,1152]{1,0:T(8,128)(2,1)} %param.4), kind=kLoop, calls=%fused_computation | loop fusion | flops 589824 | bytes 589824 | tf_op jit(solution)/shard_map/concatenate | solution.py:383
  2.9 49.2 %shard_map.59 = bf16[128,1152]{1,0:T(8,128)(2,1)S(1)} custom-call(bf16[128,1152]{1,0:T(8,128)(2,1)S(1)} %pad_maximum_fusion.raw_ref, f32[1]{0:T(128)S(6)} %copy.6.scale_ref, f32[1]{0:T(128)S(6)} %copy.7.bias_ref), custom_call_target="tpu_custom_call" | custom-call | flops 7299999744 | bytes 600000 | tf_op jit(solution)/shard_map/pallas_call | solution.py:361
  52.1 0.7 %fusion = (bf16[64,1152]{1,0:T(8,128)(2,1)}, bf16[64,1152]{1,0:T(8,128)(2,1)}) fusion(bf16[128,1152]{1,0:T(8,128)(2,1)S(1)} %shard_map.59), kind=kLoop, calls=%fused_computation.1 | loop fusion | bytes 589824 | tf_op jit(solution)/shard_map/slice | solution.py:384

commit v6 on v5

--- a/solution.py
+++ b/solution.py
@@ -177,15 +177,13 @@
     forward(0, "+", 1)
     image_step(2, 0)
     image_step(2, 1)
-    arrived("p0", "p1", "p7")
-    score(0, 384, 0, GROUP)
     image_step(2, 2)
     forward(1, "+", 1)
     image_step(2, 3)
     image_pass(2)
     image_pass(6)
-    arrived("a30", "b30", "a31", "b31")
-    score(0, 384, GROUP, GROUP)
+    arrived("p0", "p1", "p7", "a30", "b30", "a31", "b31")
+    score(0, 384, 0, 2 * GROUP)
     image_step(3, 0)
     forward(3, "-", 3)
     image_step(3, 1)

time: 53 us -> 52.6 us (level)
  no operation moved by 1% of the time
where the time goes in v6:
time: 52.6 us; the launch traced here: 52.5 us
  Pallas kernels  48.8 us (93%)
  between operations  1.93 us (4%)
  other arithmetic  1.01 us (2%)
  local copies, waits for them, and re-layouts  0.73 us (1%)
    pallas_call x1, Pallas kernels, per_device(): pl.pallas_call(kernel, out_shape=block, in_specs=[vmem, smem, smem], out_...  48.8 us

profile of v6, /device:TPU:1, one launch (start us, length us, event | category | flops | bytes accessed | tf_op | source)
XLA Modules:
  0.0 52.5 jit_solution(3103301136109262169)
XLA Ops:
  1.9 1.0 %pad_maximum_fusion.raw_ref = bf16[128,1152]{1,0:T(8,128)(2,1)S(1)} fusion(bf16[64,1152]{1,0:T(8,128)(2,1)} %param.5, bf16[64,1152]{1,0:T(8,128)(2,1)} %param.4), kind=kLoop, calls=%fused_computation | loop fusion | flops 589824 | bytes 589824 | tf_op jit(solution)/shard_map/concatenate | solution.py:381
  2.9 48.8 %shard_map.59 = bf16[128,1152]{1,0:T(8,128)(2,1)S(1)} custom-call(bf16[128,1152]{1,0:T(8,128)(2,1)S(1)} %pad_maximum_fusion.raw_ref, f32[1]{0:T(128)S(6)} %copy.6.scale_ref, f32[1]{0:T(128)S(6)} %copy.7.bias_ref), custom_call_target="tpu_custom_call" | custom-call | flops 7299999744 | bytes 600000 | tf_op jit(solution)/shard_map/pallas_call | solution.py:359
  51.7 0.7 %fusion = (bf16[64,1152]{1,0:T(8,128)(2,1)}, bf16[64,1152]{1,0:T(8,128)(2,1)}) fusion(bf16[128,1152]{1,0:T(8,128)(2,1)S(1)} %shard_map.59), kind=kLoop, calls=%fused_computation.1 | loop fusion | bytes 589824 | tf_op jit(solution)/shard_map/slice | solution.py:382
